TPU v7x, 256 devices: a whole 4x4x8 slice. The times are simulated.
256 devices in a mesh: table: 64 (over y, z, core), col: 4 (over x).
Axes of the slice: x: 4, y: 4, z: 8, core: 2. Of those that a mesh axis runs over, the one named last changes fastest.
Arguments:
- embedding: bfloat16 [262144, 256], P('table', 'col'), may hold values from -4 to 4
- accumulator: float32 [262144, 256], P('table', 'col'), may hold values from 0.01 to 1
- pair_rows: int32 [16384, 128, 4], P(('table', 'col')), may hold values from 0 to 1023
- pair_len: int32 [16384, 128], P(('table', 'col')), may hold values from 0 to 4
- pair_dest: int32 [256, 64], P(('table', 'col')), may hold values from 0 to 63, each once within a row
- pair_tile: int32 [256, 64], P(('table', 'col')), may hold values from 0 to 15
- pooled_grad: bfloat16 [524288, 256], P(('table', 'col')), may hold values from -6 to 6
Outputs:
- pooled: bfloat16 [524288, 256], P(('table', 'col'))
- new_embedding: bfloat16 [262144, 256], P(('table', 'col'))
- new_accumulator: float32 [262144, 256], P(('table', 'col'))
Inputs may be any that keep to these rules, and one draw needn't show every extreme that they name: `pair_dest`: each row names every table index exactly once.
All inputs are finite; a program needn't handle non-finite values.
Results may differ from a plain program's by a relative error of at most 0.0049.
Values may be sent and summed in bfloat16 or wider, within the bound.
A program may use at most 128 MiB of HBM per device.

v0:
```python
import jax
import jax.numpy as jnp
from jax import lax
from jax.sharding import PartitionSpec as P

LEARN_RATE = 0.3
EPSILON = 1e-08


def incidence(rows, lengths, width):
    valid = jnp.arange(rows.shape[-1], dtype=jnp.int32)[None, None, :] < lengths[:, :, None]
    hits = (rows[..., None] == jnp.arange(width, dtype=jnp.int32)) & valid[..., None]
    return jnp.sum(hits.astype(jnp.bfloat16), axis=2)


def move_state(accumulator):
    return lax.all_to_all(
        accumulator.astype(jnp.bfloat16), "col", split_axis=0, concat_axis=1, tiled=True
    ).astype(accumulator.dtype)


def per_device(embedding, accumulator, pair_rows, pair_len, pair_dest, pair_tile, pooled_grad):
    table_count = lax.axis_size("table")
    pair_count = pair_rows.shape[0]
    bag_rows = pair_rows.shape[1]
    width = embedding.shape[1] * lax.axis_size("col")
    tile_count = pooled_grad.shape[0] // bag_rows
    span = min(8, pair_count)
    groups = pair_count // span
    owned = lax.all_to_all(embedding, "col", split_axis=0, concat_axis=1, tiled=True)
    state = move_state(accumulator)
    row_count = owned.shape[0]
    rows_grouped = pair_rows.reshape(groups, span, bag_rows, pair_rows.shape[2])
    lens_grouped = pair_len.reshape(groups, span, bag_rows)
    dest_onehot = (
        pair_dest[0][None, :] == jnp.arange(table_count, dtype=jnp.int32)[:, None]
    ).astype(jnp.bfloat16)
    tile_marks = (pair_tile[0] + 1).astype(jnp.bfloat16)[:, None]
    send_tiles = jnp.dot(dest_onehot, tile_marks, preferred_element_type=jnp.float32).astype(
        jnp.bfloat16
    )
    tile_numbers = jnp.arange(tile_count, dtype=jnp.float32) + 1.0
    grad_tiles = pooled_grad.reshape(tile_count, bag_rows, width)

    def pool_group(item):
        rows, lengths = item
        counts = incidence(rows, lengths, row_count)
        part = jnp.einsum("gbr,rd->gbd", counts, owned, preferred_element_type=jnp.float32)
        return (part.astype(jnp.bfloat16), counts)

    partial_value, saved_counts = lax.map(pool_group, (rows_grouped, lens_grouped))
    partial_value = partial_value.reshape(pair_count, bag_rows, width)
    send_blocks = jnp.einsum(
        "np,pbd->nbd", dest_onehot, partial_value, preferred_element_type=jnp.float32
    ).astype(jnp.bfloat16)
    arrived, arrived_tiles = (
        lax.all_to_all(send_blocks, "table", split_axis=0, concat_axis=0, tiled=True),
        lax.all_to_all(send_tiles, "table", split_axis=0, concat_axis=0, tiled=True),
    )
    tile_onehot = (
        arrived_tiles[:, 0].astype(jnp.float32)[None, :] == tile_numbers[:, None]
    ).astype(jnp.bfloat16)
    back_blocks = jnp.einsum(
        "tn,tbd->nbd", tile_onehot, grad_tiles, preferred_element_type=jnp.float32
    ).astype(jnp.bfloat16)
    pooled = jnp.einsum("tn,nbd->tbd", tile_onehot, arrived, preferred_element_type=jnp.float32)
    pooled = pooled.astype(jnp.bfloat16).reshape(tile_count * bag_rows, width)
    returned = lax.all_to_all(back_blocks, "table", split_axis=0, concat_axis=0, tiled=True)
    pair_grads = jnp.einsum(
        "np,nbd->pbd", dest_onehot, returned, preferred_element_type=jnp.float32
    ).astype(jnp.bfloat16)
    pair_grads = pair_grads.reshape(groups, span, bag_rows, width)

    def add_group(total, item):
        counts, grads = item
        return (
            total + jnp.einsum("gbr,gbd->rd", counts, grads, preferred_element_type=jnp.float32),
            None,
        )

    empty = jnp.zeros((row_count, width), jnp.float32)
    grad, unused = lax.scan(add_group, empty, (saved_counts, pair_grads))
    new_state = state + grad * grad
    new_rows = (
        owned.astype(jnp.float32) - LEARN_RATE * grad / (jnp.sqrt(new_state) + EPSILON)
    ).astype(jnp.bfloat16)
    return (pooled, new_rows, new_state)


def solution(mesh):
    return jax.shard_map(
        per_device,
        mesh=mesh,
        in_specs=(
            P("table", "col"),
            P("table", "col"),
            P(("table", "col"), None, None),
            P(("table", "col"), None),
            P(("table", "col"), None),
            P(("table", "col"), None),
            P(("table", "col"), None),
        ),
        out_specs=(P(("table", "col"), None), P(("table", "col"), None), P(("table", "col"), None)),
        check_vma=False,
    )
```

profile of v0, /device:TPU:1, one launch (start us, length us, event | category | flops | bytes accessed | tf_op | source)
XLA Modules:
  0.0 259.6 jit_solution(2965978162360990122)
XLA Ops:
  2.3 13.2 %all-to-all-start = ((bf16[64,1,1]{2,1,0:T(2,128)(2,1)}), bf16[64,1,1]{2,1,0:T(2,128)(2,1)S(1)}, u32[]{:S(2)}, u32[]{:S(2)}) async-start(bf16[64,1,1]{2,1,0:T(2,128)(2,1)} %copy.86), calls=%async_computation | async-start | bytes 65536 | tf_op jit(solution)/shard_map/all_to_all | solution.py:58
  15.5 1.9 copy.137
  17.4 7.3 %all-to-all-done = bf16[64,1,1]{2,1,0:T(2,128)(2,1)S(1)} async-done(((bf16[64,1,1]{2,1,0:T(2,128)(2,1)}), bf16[64,1,1]{2,1,0:T(2,128)(2,1)S(1)}, u32[]{:S(2)}, u32[]{:S(2)}) %all-to-all-start) | async-done | bytes 160 | tf_op jit(solution)/shard_map/all_to_all | solution.py:58
  24.7 4.0 %all-to-all-start.1 = ((bf16[4,1024,64]{1,2,0:T(8,128)(2,1)}), bf16[4,1024,64]{1,2,0:T(8,128)(2,1)S(1)}, u32[]{:S(2)}, u32[]{:S(2)}) async-start(bf16[4,1024,64]{1,2,0:T(8,128)(2,1)} %bitcast.77), calls=%async_computation.1 | async-start | bytes 1048576 | tf_op jit(solution)/shard_map/all_to_all | solution.py:30
  28.7 1.3 convert_element_type.78
  30.8 6.2 %all-to-all-done.1 = bf16[4,1024,64]{1,2,0:T(8,128)(2,1)S(1)} async-done(((bf16[4,1024,64]{1,2,0:T(8,128)(2,1)}), bf16[4,1024,64]{1,2,0:T(8,128)(2,1)S(1)}, u32[]{:S(2)}, u32[]{:S(2)}) %all-to-all-start.1) | async-done | bytes 524320 | tf_op jit(solution)/shard_map/all_to_all | solution.py:30
  37.0 3.5 %all-to-all-start.4 = ((bf16[4,1024,64]{1,2,0:T(8,128)(2,1)}), bf16[4,1024,64]{1,2,0:T(8,128)(2,1)S(1)}, u32[]{:S(2)}, u32[]{:S(2)}) async-start(bf16[4,1024,64]{1,2,0:T(8,128)(2,1)} %bitcast.76), calls=%async_computation.4 | async-start | bytes 1048576 | tf_op jit(solution)/shard_map/all_to_all | solution.py:17
  41.0 1.4 convolution_convert_fusion.1
  42.4 4.4 %copy.97 = bf16[64,128,256]{2,1,0:T(8,128)(2,1)} copy(bf16[64,128,256]{2,0,1:T(8,128)(2,1)S(1)} %convolution_convert_fusion.1) | data formatting | bytes 8388608 | tf_op jit(solution)/shard_map/convert_element_type | solution.py:65
  47.5 8.4 %all-to-all-start.3 = ((bf16[64,128,256]{2,1,0:T(8,128)(2,1)}), bf16[64,128,256]{2,1,0:T(8,128)(2,1)}, u32[]{:S(2)}, u32[]{:S(2)}) async-start(bf16[64,128,256]{2,1,0:T(8,128)(2,1)} %copy.97), calls=%async_computation.3 | async-start | bytes 8388608 | tf_op jit(solution)/shard_map/all_to_all | solution.py:68
  55.9 67.5 %while.25 = (s32[]{:T(128)}, bf16[8,8,128,256]{3,2,1,0:T(8,128)(2,1)}, bf16[8,8,128,1024]{3,2,1,0:T(8,128)(2,1)}, s32[8,8,128,4]{2,3,1,0:T(4,128)}, s32[8,8,128]...) while((s32[]{:T(128)}, bf16[8,8,128,256]{3,2,1,0:T(8,128)(2,1)}, ...), condition=%wide.region_2.3_spmd, body=%wide.region_0.2_spmd.sunk | while | flops 552865792 | bytes 9572453 | solution.py:51
  57.4 4.0 %fusion.59 = bf16[8,128,1024]{2,1,0:T(8,128)(2,1)S(1)} fusion(s32[8,128,4]{1,2,0:T(4,128)S(1)} %copy.142, pred[8,128,4]{1,2,0:T(4,128)(4,1)S(1)} %iota_compare_fusion.5), kind=kLoop, calls=%fused_computation.3.clone.1 | loop fusion | flops 15728640 | bytes 2117632 | tf_op jit(solution)/shard_map/while/body/eval_jaxpr/reduce_sum | solution.py:13
  61.4 1.6 fusion.60
  62.9 1.5 bitcast_dynamic-update-slice_fusion.2
  65.9 4.0 %fusion.59 = bf16[8,128,1024]{2,1,0:T(8,128)(2,1)S(1)} fusion(s32[8,128,4]{1,2,0:T(4,128)S(1)} %copy.142, pred[8,128,4]{1,2,0:T(4,128)(4,1)S(1)} %iota_compare_fusion.5), kind=kLoop, calls=%fused_computation.3.clone.1 | loop fusion | flops 15728640 | bytes 2117632 | tf_op jit(solution)/shard_map/while/body/eval_jaxpr/reduce_sum | solution.py:13
  69.8 1.6 fusion.60
  71.4 1.5 bitcast_dynamic-update-slice_fusion.2
  74.3 4.0 %fusion.59 = bf16[8,128,1024]{2,1,0:T(8,128)(2,1)S(1)} fusion(s32[8,128,4]{1,2,0:T(4,128)S(1)} %copy.142, pred[8,128,4]{1,2,0:T(4,128)(4,1)S(1)} %iota_compare_fusion.5), kind=kLoop, calls=%fused_computation.3.clone.1 | loop fusion | flops 15728640 | bytes 2117632 | tf_op jit(solution)/shard_map/while/body/eval_jaxpr/reduce_sum | solution.py:13
  78.3 1.5 fusion.60
  79.8 1.5 bitcast_dynamic-update-slice_fusion.2
  82.7 4.0 %fusion.59 = bf16[8,128,1024]{2,1,0:T(8,128)(2,1)S(1)} fusion(s32[8,128,4]{1,2,0:T(4,128)S(1)} %copy.142, pred[8,128,4]{1,2,0:T(4,128)(4,1)S(1)} %iota_compare_fusion.5), kind=kLoop, calls=%fused_computation.3.clone.1 | loop fusion | flops 15728640 | bytes 2117632 | tf_op jit(solution)/shard_map/while/body/eval_jaxpr/reduce_sum | solution.py:13
  86.7 1.5 fusion.60
  88.2 1.5 bitcast_dynamic-update-slice_fusion.2
  91.1 4.0 %fusion.59 = bf16[8,128,1024]{2,1,0:T(8,128)(2,1)S(1)} fusion(s32[8,128,4]{1,2,0:T(4,128)S(1)} %copy.142, pred[8,128,4]{1,2,0:T(4,128)(4,1)S(1)} %iota_compare_fusion.5), kind=kLoop, calls=%fused_computation.3.clone.1 | loop fusion | flops 15728640 | bytes 2117632 | tf_op jit(solution)/shard_map/while/body/eval_jaxpr/reduce_sum | solution.py:13
  95.1 1.5 fusion.60
  96.6 1.5 bitcast_dynamic-update-slice_fusion.2
  99.6 4.0 %fusion.59 = bf16[8,128,1024]{2,1,0:T(8,128)(2,1)S(1)} fusion(s32[8,128,4]{1,2,0:T(4,128)S(1)} %copy.142, pred[8,128,4]{1,2,0:T(4,128)(4,1)S(1)} %iota_compare_fusion.5), kind=kLoop, calls=%fused_computation.3.clone.1 | loop fusion | flops 15728640 | bytes 2117632 | tf_op jit(solution)/shard_map/while/body/eval_jaxpr/reduce_sum | solution.py:13
  103.6 1.5 fusion.60
  105.1 1.5 bitcast_dynamic-update-slice_fusion.2
  108.0 4.0 %fusion.59 = bf16[8,128,1024]{2,1,0:T(8,128)(2,1)S(1)} fusion(s32[8,128,4]{1,2,0:T(4,128)S(1)} %copy.142, pred[8,128,4]{1,2,0:T(4,128)(4,1)S(1)} %iota_compare_fusion.5), kind=kLoop, calls=%fused_computation.3.clone.1 | loop fusion | flops 15728640 | bytes 2117632 | tf_op jit(solution)/shard_map/while/body/eval_jaxpr/reduce_sum | solution.py:13
  112.0 1.5 fusion.60
  113.5 1.5 bitcast_dynamic-update-slice_fusion.2
  116.4 4.0 %fusion.59 = bf16[8,128,1024]{2,1,0:T(8,128)(2,1)S(1)} fusion(s32[8,128,4]{1,2,0:T(4,128)S(1)} %copy.142, pred[8,128,4]{1,2,0:T(4,128)(4,1)S(1)} %iota_compare_fusion.5), kind=kLoop, calls=%fused_computation.3.clone.1 | loop fusion | flops 15728640 | bytes 2117632 | tf_op jit(solution)/shard_map/while/body/eval_jaxpr/reduce_sum | solution.py:13
  120.4 1.5 fusion.60
  121.9 1.5 bitcast_dynamic-update-slice_fusion.2
  123.4 5.5 %fusion.22 = bf16[64,128,256]{2,0,1:T(8,128)(2,1)S(1)} fusion(bf16[64,128,256]{2,1,0:T(8,128)(2,1)} %bitcast.98, s32[64]{0:T(128)S(1)} %bitcast.106), kind=kOutput, calls=%fused_computation.28 | convolution fusion | flops 270536704 | bytes 8388864 | tf_op jit(solution)/shard_map/np,pbd->nbd/dot_general | solution.py:53
  128.9 4.4 %copy.93 = bf16[64,128,256]{2,1,0:T(8,128)(2,1)} copy(bf16[64,128,256]{2,0,1:T(8,128)(2,1)S(1)} %fusion.22) | data formatting | bytes 8388608 | tf_op jit(solution)/shard_map/convert_element_type | solution.py:55
  133.3 18.6 %all-to-all-done.3 = bf16[64,128,256]{2,1,0:T(8,128)(2,1)} async-done(((bf16[64,128,256]{2,1,0:T(8,128)(2,1)}), bf16[64,128,256]{2,1,0:T(8,128)(2,1)}, u32[]{:S(2)}, u32[]{:S(2)}) %all-to-all-start.3) | async-done | bytes 4194336 | tf_op jit(solution)/shard_map/all_to_all | solution.py:68
  151.9 6.0 %all-to-all-start.2 = ((bf16[64,128,256]{2,1,0:T(8,128)(2,1)}), bf16[64,128,256]{2,1,0:T(8,128)(2,1)}, u32[]{:S(2)}, u32[]{:S(2)}) async-start(bf16[64,128,256]{2,1,0:T(8,128)(2,1)} %copy.93), calls=%async_computation.2 | async-start | bytes 8388608 | tf_op jit(solution)/shard_map/all_to_all | solution.py:57
  157.9 7.4 %convert_bitcast_fusion = bf16[8,8,128,256]{3,1,0,2:T(8,128)(2,1)} fusion(bf16[64,128,256]{2,1,0:T(8,128)(2,1)} %all-to-all-done.3, s32[64]{0:T(128)S(1)} %bitcast.107), kind=kOutput, calls=%fused_computation.27 | convolution fusion | flops 270536704 | bytes 8388864 | tf_op jit(solution)/shard_map/np,nbd->pbd/dot_general | solution.py:69
  165.3 37.3 %while.26 = (s32[]{:T(128)}, f32[1024,256]{1,0:T(8,128)}, bf16[8,8,128,1024]{3,2,1,0:T(8,128)(2,1)}, bf16[8,8,128,256]{3,1,0,2:T(8,128)(2,1)}, s32[]{:T(128)}, /*index=5*/s32[]{:T(128)}) while((s32[]{:T(128)}, f32[1024,256]{1,0:T(8,128)}, bf16[8,8,128,1024]{3,2,1,0:T(8,128)(2,1)}, bf16[8,8,128,256]{3,1,0,2:T(8,128)(2,1)}, ...), condition=%wide.region_4.5_spmd.clone, body=%wide.region_3.4_spmd.clone.sunk | while | flops 537395200 | bytes 5767263 | solution.py:82
  165.3 1.1 constant_dynamic-slice_fusion.5
  166.4 3.3 %fusion.62 = f32[1024,256]{1,0:T(8,128)} fusion(bf16[8,8,128,1024]{3,2,1,0:T(8,128)(2,1)} %get-tuple-element.309, s32[]{:T(128)S(6)} %copy.157, f32[1024,256]{1,0:T(8,128)} %get-tuple-element.302, bf16[1,8,128,256]{3,1,0,2:T(8,128)(2,1)S(1)} %constant_dynamic-slice_fusion.5, pred[]{:T(512)S(6)} %compare.3), kind=kOutput, calls=%fused_computation.17.clone.1 | convolution fusion | flops 537395200 | bytes 4718597 | tf_op jit(solution)/shard_map/while/body/eval_jaxpr/gbr,gbd->rd/dot_general | solution.py:77
  169.7 1.1 constant_dynamic-slice_fusion.5
  170.8 3.6 %fusion.62 = f32[1024,256]{1,0:T(8,128)} fusion(bf16[8,8,128,1024]{3,2,1,0:T(8,128)(2,1)} %get-tuple-element.309, s32[]{:T(128)S(6)} %copy.157, f32[1024,256]{1,0:T(8,128)} %get-tuple-element.302, bf16[1,8,128,256]{3,1,0,2:T(8,128)(2,1)S(1)} %constant_dynamic-slice_fusion.5, pred[]{:T(512)S(6)} %compare.3), kind=kOutput, calls=%fused_computation.17.clone.1 | convolution fusion | flops 537395200 | bytes 4718597 | tf_op jit(solution)/shard_map/while/body/eval_jaxpr/gbr,gbd->rd/dot_general | solution.py:77
  174.4 1.1 constant_dynamic-slice_fusion.5
  175.5 3.6 %fusion.62 = f32[1024,256]{1,0:T(8,128)} fusion(bf16[8,8,128,1024]{3,2,1,0:T(8,128)(2,1)} %get-tuple-element.309, s32[]{:T(128)S(6)} %copy.157, f32[1024,256]{1,0:T(8,128)} %get-tuple-element.302, bf16[1,8,128,256]{3,1,0,2:T(8,128)(2,1)S(1)} %constant_dynamic-slice_fusion.5, pred[]{:T(512)S(6)} %compare.3), kind=kOutput, calls=%fused_computation.17.clone.1 | convolution fusion | flops 537395200 | bytes 4718597 | tf_op jit(solution)/shard_map/while/body/eval_jaxpr/gbr,gbd->rd/dot_general | solution.py:77
  179.1 1.1 constant_dynamic-slice_fusion.5
  180.2 3.6 %fusion.62 = f32[1024,256]{1,0:T(8,128)} fusion(bf16[8,8,128,1024]{3,2,1,0:T(8,128)(2,1)} %get-tuple-element.309, s32[]{:T(128)S(6)} %copy.157, f32[1024,256]{1,0:T(8,128)} %get-tuple-element.302, bf16[1,8,128,256]{3,1,0,2:T(8,128)(2,1)S(1)} %constant_dynamic-slice_fusion.5, pred[]{:T(512)S(6)} %compare.3), kind=kOutput, calls=%fused_computation.17.clone.1 | convolution fusion | flops 537395200 | bytes 4718597 | tf_op jit(solution)/shard_map/while/body/eval_jaxpr/gbr,gbd->rd/dot_general | solution.py:77
  183.8 1.1 constant_dynamic-slice_fusion.5
  184.9 3.6 %fusion.62 = f32[1024,256]{1,0:T(8,128)} fusion(bf16[8,8,128,1024]{3,2,1,0:T(8,128)(2,1)} %get-tuple-element.309, s32[]{:T(128)S(6)} %copy.157, f32[1024,256]{1,0:T(8,128)} %get-tuple-element.302, bf16[1,8,128,256]{3,1,0,2:T(8,128)(2,1)S(1)} %constant_dynamic-slice_fusion.5, pred[]{:T(512)S(6)} %compare.3), kind=kOutput, calls=%fused_computation.17.clone.1 | convolution fusion | flops 537395200 | bytes 4718597 | tf_op jit(solution)/shard_map/while/body/eval_jaxpr/gbr,gbd->rd/dot_general | solution.py:77
  188.5 1.1 constant_dynamic-slice_fusion.5
  189.6 3.6 %fusion.62 = f32[1024,256]{1,0:T(8,128)} fusion(bf16[8,8,128,1024]{3,2,1,0:T(8,128)(2,1)} %get-tuple-element.309, s32[]{:T(128)S(6)} %copy.157, f32[1024,256]{1,0:T(8,128)} %get-tuple-element.302, bf16[1,8,128,256]{3,1,0,2:T(8,128)(2,1)S(1)} %constant_dynamic-slice_fusion.5, pred[]{:T(512)S(6)} %compare.3), kind=kOutput, calls=%fused_computation.17.clone.1 | convolution fusion | flops 537395200 | bytes 4718597 | tf_op jit(solution)/shard_map/while/body/eval_jaxpr/gbr,gbd->rd/dot_general | solution.py:77
  193.2 1.1 constant_dynamic-slice_fusion.5
  194.2 3.6 %fusion.62 = f32[1024,256]{1,0:T(8,128)} fusion(bf16[8,8,128,1024]{3,2,1,0:T(8,128)(2,1)} %get-tuple-element.309, s32[]{:T(128)S(6)} %copy.157, f32[1024,256]{1,0:T(8,128)} %get-tuple-element.302, bf16[1,8,128,256]{3,1,0,2:T(8,128)(2,1)S(1)} %constant_dynamic-slice_fusion.5, pred[]{:T(512)S(6)} %compare.3), kind=kOutput, calls=%fused_computation.17.clone.1 | convolution fusion | flops 537395200 | bytes 4718597 | tf_op jit(solution)/shard_map/while/body/eval_jaxpr/gbr,gbd->rd/dot_general | solution.py:77
  197.8 1.1 constant_dynamic-slice_fusion.5
  198.9 3.6 %fusion.62 = f32[1024,256]{1,0:T(8,128)} fusion(bf16[8,8,128,1024]{3,2,1,0:T(8,128)(2,1)} %get-tuple-element.309, s32[]{:T(128)S(6)} %copy.157, f32[1024,256]{1,0:T(8,128)} %get-tuple-element.302, bf16[1,8,128,256]{3,1,0,2:T(8,128)(2,1)S(1)} %constant_dynamic-slice_fusion.5, pred[]{:T(512)S(6)} %compare.3), kind=kOutput, calls=%fused_computation.17.clone.1 | convolution fusion | flops 537395200 | bytes 4718597 | tf_op jit(solution)/shard_map/while/body/eval_jaxpr/gbr,gbd->rd/dot_general | solution.py:77
  202.5 2.5 copy.101
  205.1 2.6 bitcast_add_fusion
  207.7 2.0 copy.105
  209.7 1.3 copy.106
  211.0 42.7 %all-to-all-done.2 = bf16[64,128,256]{2,1,0:T(8,128)(2,1)} async-done(((bf16[64,128,256]{2,1,0:T(8,128)(2,1)}), bf16[64,128,256]{2,1,0:T(8,128)(2,1)}, u32[]{:S(2)}, u32[]{:S(2)}) %all-to-all-start.2) | async-done | bytes 4194336 | tf_op jit(solution)/shard_map/all_to_all | solution.py:57
  253.7 4.5 %fusion.27 = bf16[16,128,256]{2,0,1:T(8,128)(2,1)S(1)} fusion(bf16[64,128,256]{2,1,0:T(8,128)(2,1)} %all-to-all-done.2, f32[64]{0:T(128)S(1)} %convert_reduce_fusion, f32[16]{0:T(128)S(1)} %iota_add_fusion), kind=kOutput, calls=%fused_computation.30 | convolution fusion | flops 67634176 | bytes 5243200 | tf_op jit(solution)/shard_map/tn,nbd->tbd/dot_general | solution.py:66
  258.3 1.3 copy.95
  (54 shorter events, 15.3 us)
Async XLA Ops:
  0.6 40.4 %copy-start = (bf16[2048,256]{1,0:T(8,128)(2,1)S(1)}, bf16[2048,256]{1,0:T(8,128)(2,1)}, u32[]{:S(2)}) copy-start(bf16[2048,256]{1,0:T(8,128)(2,1)} %param.17) | copy-start | bytes 3145732
  2.3 22.4 %all-to-all-start = ((bf16[64,1,1]{2,1,0:T(2,128)(2,1)}), bf16[64,1,1]{2,1,0:T(2,128)(2,1)S(1)}, u32[]{:S(2)}, u32[]{:S(2)}) async-start(bf16[64,1,1]{2,1,0:T(2,128)(2,1)} %copy.86), calls=%async_computation | async-start | bytes 65536 | tf_op jit(solution)/shard_map/all_to_all | solution.py:58
  24.7 12.3 %all-to-all-start.1 = ((bf16[4,1024,64]{1,2,0:T(8,128)(2,1)}), bf16[4,1024,64]{1,2,0:T(8,128)(2,1)S(1)}, u32[]{:S(2)}, u32[]{:S(2)}) async-start(bf16[4,1024,64]{1,2,0:T(8,128)(2,1)} %bitcast.77), calls=%async_computation.1 | async-start | bytes 1048576 | tf_op jit(solution)/shard_map/all_to_all | solution.py:30
  37.0 10.5 %all-to-all-start.4 = ((bf16[4,1024,64]{1,2,0:T(8,128)(2,1)}), bf16[4,1024,64]{1,2,0:T(8,128)(2,1)S(1)}, u32[]{:S(2)}, u32[]{:S(2)}) async-start(bf16[4,1024,64]{1,2,0:T(8,128)(2,1)} %bitcast.76), calls=%async_computation.4 | async-start | bytes 1048576 | tf_op jit(solution)/shard_map/all_to_all | solution.py:17
  47.5 104.3 %all-to-all-start.3 = ((bf16[64,128,256]{2,1,0:T(8,128)(2,1)}), bf16[64,128,256]{2,1,0:T(8,128)(2,1)}, u32[]{:S(2)}, u32[]{:S(2)}) async-start(bf16[64,128,256]{2,1,0:T(8,128)(2,1)} %copy.97), calls=%async_computation.3 | async-start | bytes 8388608 | tf_op jit(solution)/shard_map/all_to_all | solution.py:68
  55.9 67.5 %copy-start.1 = (s32[1,64]{1,0:T(1,128)S(1)}, s32[1,64]{1,0:T(1,128)}, u32[]{:S(2)}) copy-start(s32[1,64]{1,0:T(1,128)} %param.15) | copy-start | bytes 772
  151.9 101.9 %all-to-all-start.2 = ((bf16[64,128,256]{2,1,0:T(8,128)(2,1)}), bf16[64,128,256]{2,1,0:T(8,128)(2,1)}, u32[]{:S(2)}, u32[]{:S(2)}) async-start(bf16[64,128,256]{2,1,0:T(8,128)(2,1)} %copy.93), calls=%async_computation.2 | async-start | bytes 8388608 | tf_op jit(solution)/shard_map/all_to_all | solution.py:57
where the time goes:
time: 261 us; the launch traced here: 260 us
  waiting for transfers between devices  75.3 us (29%)
  matrix products  60.5 us (23%)
  local copies, waits for them, and re-layouts  51.6 us (20%)
  other arithmetic  36.2 us (14%)
  starting transfers between devices  35.1 us (13%)
    all_to_all x1, waiting for transfers between devices, per_device(): lax.all_to_all(send_blocks, 'table', split_axis=0, concat_axis=0, tiled=T...  42.7 us
    reduce_sum x8, other arithmetic, incidence(): return jnp.sum(hits.astype(jnp.bfloat16), axis=2)  31.6 us
    dot_general x8, matrix products, add_group(): jnp.einsum('gbr,gbd->rd', counts, grads, preferred_element_type=jnp.float32)  28.6 us
    all_to_all x1, waiting for transfers between devices, per_device(): lax.all_to_all(back_blocks, 'table', split_axis=0, concat_axis=0, tiled=T...  18.6 us
    all_to_all x1, starting transfers between devices, per_device(): lax.all_to_all(send_tiles, 'table', split_axis=0, concat_axis=0, tiled=True)  13.2 us
    dot_general x8, matrix products, pool_group(): jnp.einsum('gbr,rd->gbd', counts, owned, preferred_element_type=jnp.float32)  12.2 us
    dynamic_update_slice x8, local copies, waits for them, and re-layouts, per_device(): lax.map(pool_group, (rows_grouped, lens_grouped))  12 us
    dynamic_slice x8, local copies, waits for them, and re-layouts, per_device(): grad, unused = lax.scan(add_group, empty, (saved_counts, pair_grads))  8.6 us
  transfers between devices with their start and end apart: 5, of which 5 were waited for; matrix products, arithmetic and copies ran while one was open for 54% of the time, Pallas kernels for 0%

commit v1 on v0

v1 whole, which is shorter than its diff:
```python
import functools
import jax
import jax.numpy as jnp
from jax import lax
from jax.experimental import pallas as pl
from jax.experimental.pallas import tpu as pltpu
from jax.sharding import PartitionSpec as P

LEARN_RATE = 0.3
EPSILON = 1e-08
MESH = pl.DeviceIdType.MESH
NY, NZ, NCORE, NX = 4, 8, 2, 4
PLANE = NY * NCORE
ROWS = 1024
DIM = 256
BAGS = 128
LOOK = 4
TILES = 16
FEAT = DIM // NX
SPAN = PLANE * BAGS
TILE_UNIT = 2048
HALF = DIM // 2


def prep_kernel(dest_ref, tile_ref, rows_ref, len_ref, msg_ref):
    look = lax.broadcasted_iota(jnp.int32, (LOOK, BAGS), 0)

    def one(pair, carry):
        dest = dest_ref[0, pair]
        place = (dest // NCORE) % NZ * PLANE + dest // (NCORE * NZ) * NCORE + dest % NCORE
        valid = look < len_ref[pl.ds(pair, 1), :]
        msg_ref[place] = jnp.where(valid, rows_ref[pair], ROWS) + tile_ref[0, pair] * TILE_UNIT
        return carry

    lax.fori_loop(0, NZ * PLANE, one, 0)


def move_kernel(
    emb_ref, acc_ref, msg_ref, cot_ref,
    arr_ref, tiles_ref, grad_ref, own_ref, state_ref,
    emb_all, counts, cot_all, part, tile_rows, idx, gsend, grecv, gsum, chosen, acc_half, acc_own, row_ids, tile_nums,
    ex_s, ex_r, ax_s, ax_r, ix_s, ix_r, e_s, e_r, cy_s, cy_r, cx_s, cx_r, p_s, p_r, t_s, t_r, g_s, g_r, loc,
):
    t = lax.axis_index("table")
    x = lax.axis_index("col")
    y, z, core = t // (NZ * NCORE), (t // NCORE) % NZ, t % NCORE

    def at(yy, zz, cc):
        return (lax.rem(yy + NY, NY) * NZ + lax.rem(zz + NZ, NZ)) * NCORE + lax.rem(cc + NCORE, NCORE)

    def plane(zz):
        return lax.rem(zz + 2 * NZ, NZ)

    def spot(yy, cc):
        return lax.rem(yy + NY, NY) * NCORE + lax.rem(cc + NCORE, NCORE)

    me = spot(y, core)
    others = [(dy, dc) for dy in (2, 1, 3, 0) for dc in (0, 1) if (dy, dc) != (0, 0)]

    barrier = pltpu.get_barrier_semaphore()
    for j in range(1, NX):
        pl.semaphore_signal(barrier, inc=1, device_id=(t, lax.rem(x + j, NX)), device_id_type=MESH)
    for j in range(1, NZ):
        pl.semaphore_signal(barrier, inc=1, device_id=(at(y, z + j, core), x), device_id_type=MESH)
    for dy, dc in others:
        pl.semaphore_signal(barrier, inc=1, device_id=(at(y + dy, z, core + dc), x), device_id_type=MESH)
    pl.semaphore_wait(barrier, NX - 1 + NZ - 1 + PLANE - 1)

    sent = []

    def send(src, dst, send_sem, recv_sem, table, col):
        copy = pltpu.make_async_remote_copy(
            src_ref=src, dst_ref=dst, send_sem=send_sem, recv_sem=recv_sem, device_id=(table, col), device_id_type=MESH
        )
        copy.start()
        sent.append(copy)

    def arrived(dst, recv_sem):
        pltpu.make_async_copy(dst, dst, recv_sem).wait()

    def feature_rows(q):
        return pl.ds(pl.multiple_of(q * FEAT, FEAT), FEAT)

    def lanes(start, size):
        return pl.ds(pl.multiple_of(start, 128), size)

    for j in range(1, NX):
        owner = lax.rem(x + j, NX)
        send(
            emb_ref.at[:, lanes(owner * ROWS, ROWS)], emb_all.at[z, feature_rows(x)],
            ex_s.at[j - 1], ex_r.at[j - 1], t, owner,
        )
    emb_all[z, feature_rows(x), :] = emb_ref[:, lanes(x * ROWS, ROWS)]

    def pass_rows(way, step, order, q):
        source = plane(z - step) if way == 0 else plane(z + step)
        target = plane(z + 1) if way == 0 else plane(z - 1)
        block = emb_all.at[source, feature_rows(q)]
        send(block, block, e_s.at[way, step, order], e_r.at[way, step + 1, order], at(y, target, core), x)

    def wait_rows(way, step, order, q):
        source = plane(z - step) if way == 0 else plane(z + step)
        arrived(emb_all.at[source, feature_rows(q)], e_r.at[way, step, order])

    for way in (0, 1):
        pass_rows(way, 0, 0, x)

    for off in (1, 7, 2, 6, 3, 5, 4):
        target = plane(z + off)
        send(msg_ref.at[target], idx.at[z], ix_s.at[off], ix_r.at[off], at(y, target, core), x)

    def tiles4(c):
        return pl.ds(4 * c, 4)

    for c in range(4):
        for way, dy in ((0, 1), (1, -1)):
            c_way = c if way == 0 else (c + 2) % 4
            send(
                cot_ref.at[tiles4(c_way)], cot_all.at[me, tiles4(c_way)],
                cy_s.at[way, 0, c_way], cy_r.at[way, 1, c_way], at(y + dy, z, core), x,
            )
    for c in range(4):
        send(cot_ref.at[tiles4(c)], cot_all.at[me, tiles4(c)], cx_s.at[0, c], cx_r.at[0, c], at(y, z, core + 1), x)
    own_cot = pltpu.make_async_copy(cot_ref, cot_all.at[me], loc.at[0])
    own_cot.start()

    idx[z] = msg_ref[z]
    acc_half[...] = acc_ref[...].astype(jnp.bfloat16)

    ids = lax.broadcasted_iota(jnp.int32, (DIM, BAGS), 0)
    row_ids[...] = ids.astype(jnp.float32).astype(jnp.bfloat16)

    def build(zo):
        def pair(n, carry):
            held = idx[zo, n]
            tile_rows[n, pl.ds(zo, 1), :] = lax.shift_right_logical(held[:1], 11)
            row = held & (TILE_UNIT - 1)
            for block in range(ROWS // DIM):
                near = jnp.clip(row - block * DIM, -1, DIM).astype(jnp.float32).astype(jnp.bfloat16)
                total = None
                for l in range(LOOK):
                    hit = jnp.where(row_ids[...] == near[l : l + 1], 1.0, 0.0).astype(jnp.bfloat16)
                    total = hit if total is None else total + hit
                counts[zo, pl.ds(block * DIM, DIM), lanes(n * BAGS, BAGS)] = total
            return carry

        lax.fori_loop(0, PLANE, pair, 0)

    def pool(zo, order):
        def block(b, carry):
            got = jnp.dot(
                emb_all[zo], counts[zo, :, lanes(b * DIM, DIM)], preferred_element_type=jnp.float32
            ).astype(jnp.bfloat16)
            part[zo, 2 * b] = got[:, :BAGS]
            part[zo, 2 * b + 1] = got[:, BAGS:]
            return carry

        lax.fori_loop(0, SPAN // DIM, block, 0)
        for k, (dy, dc) in enumerate(others):
            dest = spot(y + dy, core + dc)
            send(part.at[zo, dest], arr_ref.at[me, zo], p_s.at[order, k], p_r.at[order, k], at(y + dy, z, core + dc), x)
        pltpu.make_async_copy(part.at[zo, me], arr_ref.at[me, zo], loc.at[1 + order]).start()

    build(z)
    for j in range(1, NX):
        q = lax.rem(x - j + NX, NX)
        arrived(emb_all.at[z, feature_rows(q)], ex_r.at[j - 1])
        for way in (0, 1):
            pass_rows(way, 0, j, q)
    for j in range(1, NX):
        owner = lax.rem(x + j, NX)
        send(
            acc_half.at[:, lanes(owner * ROWS, ROWS)], acc_own.at[feature_rows(x)],
            ax_s.at[j - 1], ax_r.at[j - 1], t, owner,
        )
    acc_own[feature_rows(x), :] = acc_half[:, lanes(x * ROWS, ROWS)]
    pool(z, 0)

    def relay_cot(way, step, c):
        dy = 1 if way == 0 else -1
        source = spot(y - dy * step, core)
        block = cot_all.at[source, tiles4(c)]
        arrived(block, cy_r.at[way, step, c])
        if step == 1 and c // 2 == way:
            send(block, block, cy_s.at[way, 1, c], cy_r.at[way, 2, c], at(y + dy, z, core), x)
        slot = 1 + way if step == 1 else 3
        send(block, block, cx_s.at[slot, c], cx_r.at[slot, c], at(y, z, core + 1), x)

    order = 1
    for step in range(1, NZ // 2 + 1):
        near, far = plane(z - step), plane(z + step)
        sources = ((near, step), (far, NZ - step)) if step < NZ // 2 else ((near, step),)
        for zo, off in sources:
            arrived(idx.at[zo], ix_r.at[off])
            build(zo)
        if step < NZ // 2:
            for k in range(NX):
                for way, zo in ((0, near), (1, far)):
                    if step > 1 or True:
                        q = lax.rem(x - k + NX, NX)
                        wait_rows(way, step, k, q)
                        if step < NZ // 2 - 1 or (k < NX // 2) == (way == 0):
                            pass_rows(way, step, k, q)
            if step == 1:
                for c in (0, 1):
                    relay_cot(0, 1, c)
                    relay_cot(1, 1, 2 + c)
            if step == 2:
                for c in (0, 1):
                    relay_cot(0, 1, 2 + c)
                    relay_cot(1, 1, c)
            if step == 3:
                for c in (0, 1):
                    relay_cot(0, 2, c)
                    relay_cot(1, 2, 2 + c)
        else:
            for k in range(NX):
                q = lax.rem(x - k + NX, NX)
                wait_rows(0 if k < NX // 2 else 1, step, k, q)
        for zo, off in sources:
            pool(zo, order)
            order += 1

    to_scalars = pltpu.make_async_copy(tile_rows, tile_nums, loc.at[9])
    to_scalars.start()
    for k, (dy, dc) in enumerate(others):
        dest = spot(y + dy, core + dc)
        send(tile_rows.at[dest], tiles_ref.at[me], t_s.at[k], t_r.at[k], at(y + dy, z, core + dc), x)
    tiles_ref[me] = tile_rows[me]
    to_scalars.wait()

    own_cot.wait()
    for c in range(4):
        arrived(cot_all.at[spot(y, core + 1), tiles4(c)], cx_r.at[0, c])
        arrived(cot_all.at[spot(y - 1, core + 1), tiles4(c)], cx_r.at[1, c])
        arrived(cot_all.at[spot(y + 1, core + 1), tiles4(c)], cx_r.at[2, c])
        arrived(cot_all.at[spot(y + 2, core + 1), tiles4(c)], cx_r.at[3, c])

    def gradient(zo):
        def pick(n, carry):
            chosen[pl.ds(pl.multiple_of(n * BAGS, BAGS), BAGS), :] = cot_all[n, tile_nums[n, zo, 0]]
            return carry

        lax.fori_loop(0, PLANE, pick, 0)

        def block(b, carry):
            rows = pl.ds(pl.multiple_of(b * DIM, DIM), DIM)
            gsum[rows, :] = jnp.dot(counts[zo, rows, :], chosen[...], preferred_element_type=jnp.float32)
            return carry

        lax.fori_loop(0, ROWS // DIM, block, 0)

    def pass_grad(way, dist, half, add):
        if add:
            arrived(grecv.at[way, dist, half], g_r.at[way, dist, half])

        def block(b, carry):
            rows = pl.ds(pl.multiple_of(b * DIM, DIM), DIM)
            value = gsum[rows, half * HALF : (half + 1) * HALF]
            if add:
                value = value + grecv[way, dist, half, rows, :].astype(jnp.float32)
            gsend[way, dist - 1, half, rows, :] = value.astype(jnp.bfloat16)
            return carry

        lax.fori_loop(0, ROWS // DIM, block, 0)
        target = plane(z + 1) if way == 0 else plane(z - 1)
        send(
            gsend.at[way, dist - 1, half], grecv.at[way, dist - 1, half],
            g_s.at[way, dist - 1, half], g_r.at[way, dist - 1, half], at(y, target, core), x,
        )

    gradient(plane(z + NZ // 2))
    pass_grad(0, NZ // 2, 0, False)
    pass_grad(1, NZ // 2, 1, False)
    for dist in range(NZ // 2 - 1, 0, -1):
        for way in (0, 1):
            gradient(plane(z + dist) if way == 0 else plane(z - dist))
            late = way
            if dist == NZ // 2 - 1:
                pass_grad(way, dist, 1 - late, False)
                pass_grad(way, dist, late, True)
            else:
                pass_grad(way, dist, 0, True)
                pass_grad(way, dist, 1, True)
    gradient(z)

    for j in range(1, NX):
        arrived(acc_own.at[feature_rows(lax.rem(x - j + NX, NX))], ax_r.at[j - 1])

    def turn(b, carry):
        rows = pl.ds(pl.multiple_of(b * 128, 128), 128)
        own_ref[rows, :] = emb_all[z, :, rows].astype(jnp.float32).T.astype(jnp.bfloat16)
        state_ref[rows, :] = acc_own[:, rows].astype(jnp.float32).T.astype(jnp.bfloat16)
        return carry

    lax.fori_loop(0, ROWS // 128, turn, 0)

    for half in (0, 1):
        for way in (0, 1):
            arrived(grecv.at[way, 0, half], g_r.at[way, 0, half])

    def total(b, carry):
        rows = pl.ds(pl.multiple_of(b * DIM, DIM), DIM)
        for half in (0, 1):
            cols = slice(half * HALF, (half + 1) * HALF)
            grad_ref[rows, cols] = (
                gsum[rows, cols]
                + grecv[0, 0, half, rows, :].astype(jnp.float32)
                + grecv[1, 0, half, rows, :].astype(jnp.float32)
            )
        return carry

    lax.fori_loop(0, ROWS // DIM, total, 0)

    order = 0
    for step in range(NZ // 2 + 1):
        for zo in (plane(z - step), plane(z + step)) if 0 < step < NZ // 2 else (plane(z - step),):
            for k, (dy, dc) in enumerate(others):
                arrived(arr_ref.at[spot(y - dy, core - dc), zo], p_r.at[order, k])
            pltpu.make_async_copy(part.at[zo, me], arr_ref.at[me, zo], loc.at[1 + order]).wait()
            order += 1
    for k, (dy, dc) in enumerate(others):
        arrived(tiles_ref.at[spot(y - dy, core - dc)], t_r.at[k])
    for copy in sent:
        copy.wait_send()


def finish_kernel(tiles_ref, arr_ref, grad_ref, own_ref, state_ref, pooled_ref, rows_ref, sums_ref, total):
    step = pl.program_id(0)

    @pl.when(step == 0)
    def _():
        total[...] = jnp.zeros_like(total)

    def add(k, carry):
        tile = tiles_ref[step, k, 0]
        total[tile] = total[tile] + arr_ref[0, k].astype(jnp.float32)
        return carry

    lax.fori_loop(0, NZ, add, 0)
    grad = grad_ref[...]
    new_state = state_ref[...].astype(jnp.float32) + grad * grad
    sums_ref[...] = new_state
    rows_ref[...] = (
        own_ref[...].astype(jnp.float32) - LEARN_RATE * grad / (jnp.sqrt(new_state) + EPSILON)
    ).astype(jnp.bfloat16)

    @pl.when(step == PLANE - 1)
    def _():
        def turn(k, carry):
            pooled_ref[k] = total[k].T.astype(jnp.bfloat16)
            return carry

        lax.fori_loop(0, TILES, turn, 0)


def per_device(embedding, accumulator, pair_rows, pair_len, pair_dest, pair_tile, pooled_grad):
    smem = pl.BlockSpec(memory_space=pltpu.SMEM)
    vmem = pl.BlockSpec(memory_space=pltpu.VMEM)
    hbm = pl.BlockSpec(memory_space=pl.ANY)
    bf16, f32, i32 = jnp.bfloat16, jnp.float32, jnp.int32
    msg = pl.pallas_call(
        prep_kernel,
        out_shape=jax.ShapeDtypeStruct((NZ * PLANE, LOOK, BAGS), i32),
        in_specs=[smem, smem, vmem, vmem],
        out_specs=vmem,
        name="sort_pairs",
    )(pair_dest, pair_tile, jnp.transpose(pair_rows, (0, 2, 1)), pair_len)
    msg = msg.reshape(NZ, PLANE, LOOK, BAGS)
    dma = pltpu.SemaphoreType.DMA
    sems = [(3,), (3,), (3,), (3,), (8,), (8,), (2, 5, 4), (2, 5, 4), (2, 3, 4), (2, 3, 4), (4, 4), (4, 4),
            (8, 7), (8, 7), (7,), (7,), (2, 4, 2), (2, 4, 2), (10,)]
    arr, tiles, grad, own, state = pl.pallas_call(
        move_kernel,
        out_shape=(
            jax.ShapeDtypeStruct((PLANE, NZ, DIM, BAGS), bf16),
            jax.ShapeDtypeStruct((PLANE, NZ, BAGS), i32),
            jax.ShapeDtypeStruct((ROWS, DIM), f32),
            jax.ShapeDtypeStruct((ROWS, DIM), bf16),
            jax.ShapeDtypeStruct((ROWS, DIM), bf16),
        ),
        in_specs=[vmem, vmem, vmem, hbm],
        out_specs=(hbm, vmem, vmem, vmem, vmem),
        scratch_shapes=[
            pltpu.VMEM((NZ, DIM, ROWS), bf16),
            pltpu.VMEM((NZ, ROWS, SPAN), bf16),
            pltpu.VMEM((PLANE, TILES, BAGS, DIM), bf16),
            pltpu.VMEM((NZ, PLANE, DIM, BAGS), bf16),
            pltpu.VMEM((PLANE, NZ, BAGS), i32),
            pltpu.VMEM((NZ, PLANE, LOOK, BAGS), i32),
            pltpu.VMEM((2, 4, 2, ROWS, HALF), bf16),
            pltpu.VMEM((2, 4, 2, ROWS, HALF), bf16),
            pltpu.VMEM((ROWS, DIM), f32),
            pltpu.VMEM((SPAN, DIM), bf16),
            pltpu.VMEM((FEAT, NX * ROWS), bf16),
            pltpu.VMEM((DIM, ROWS), bf16),
            pltpu.VMEM((DIM, BAGS), bf16),
            pltpu.SMEM((PLANE, NZ, BAGS), i32),
        ]
        + [dma(s) for s in sems],
        compiler_params=pltpu.CompilerParams(collective_id=0, has_side_effects=True, vmem_limit_bytes=58 << 20),
        name="move_rows_and_tiles",
    )(embedding.T, accumulator.T, msg, pooled_grad.reshape(TILES, BAGS, DIM))
    rows8 = ROWS // PLANE
    row_block = pl.BlockSpec((rows8, DIM), lambda i: (i, 0))
    pooled, new_rows, new_state = pl.pallas_call(
        finish_kernel,
        grid=(PLANE,),
        out_shape=(
            jax.ShapeDtypeStruct((TILES, BAGS, DIM), bf16),
            jax.ShapeDtypeStruct((ROWS, DIM), bf16),
            jax.ShapeDtypeStruct((ROWS, DIM), f32),
        ),
        in_specs=[smem, pl.BlockSpec((1, NZ, DIM, BAGS), lambda i: (i, 0, 0, 0)), row_block, row_block, row_block],
        out_specs=(pl.BlockSpec((TILES, BAGS, DIM), lambda i: (0, 0, 0)), row_block, row_block),
        scratch_shapes=[pltpu.VMEM((TILES, DIM, BAGS), f32)],
        compiler_params=pltpu.CompilerParams(vmem_limit_bytes=24 << 20),
        name="finish",
    )(tiles, arr, grad, own, state)
    return (pooled.reshape(TILES * BAGS, DIM), new_rows, new_state)


def solution(mesh):
    return jax.shard_map(
        per_device,
        mesh=mesh,
        in_specs=(
            P("table", "col"),
            P("table", "col"),
            P(("table", "col"), None, None),
            P(("table", "col"), None),
            P(("table", "col"), None),
            P(("table", "col"), None),
            P(("table", "col"), None),
        ),
        out_specs=(P(("table", "col"), None), P(("table", "col"), None), P(("table", "col"), None)),
        check_vma=False,
    )
```

time: 261 us -> 128 us (0.49)
  the two profiles are of different devices: /device:TPU:1 before, /device:TPU:2 now
where the time goes in v1:
time: 128 us; the launch traced here: 127 us
  Pallas kernels  120 us (94%)
  local copies, waits for them, and re-layouts  6.24 us (5%)
    pallas_call x1, Pallas kernels, per_device(): pl.pallas_call(move_kernel, out_shape=(jax.ShapeDtypeStruct((PLANE, NZ, D...  111 us
    pallas_call x1, Pallas kernels, per_device(): pl.pallas_call(finish_kernel, grid=(PLANE,), out_shape=(jax.ShapeDtypeStr...  7.05 us
    unnamed x10, local copies, waits for them, and re-layouts  6.24 us
    pallas_call x1, Pallas kernels, per_device(): pl.pallas_call(prep_kernel, out_shape=jax.ShapeDtypeStruct((NZ * PLANE, L...  2.68 us

profile of v1, /device:TPU:2, one launch (start us, length us, event | category | flops | bytes accessed | tf_op | source)
XLA Modules:
  0.0 127.3 jit_solution(5948030169363392099)
XLA Ops:
  0.6 2.7 %sort_pairs.1 = s32[64,4,128]{2,1,0:T(4,128)} custom-call(s32[1,64]{1,0:T(1,128)} %dest_ref.1, s32[1,64]{1,0:T(1,128)} %tile_ref.1, s32[64,4,128]{2,1,0:T(4,128)} %bitcast.10, s32[64,128]{1,0:T(8,128)} %len_ref.1), custom_call_target="tpu_custom_call" | custom-call | tf_op jit(solution)/shard_map/sort_pairs/pallas_call | solution.py:362
  3.3 110.7 %move_rows_and_tiles.1 = (bf16[8,8,256,128]{3,2,1,0:T(8,128)(2,1)}, s32[8,8,128]{2,1,0:T(8,128)}, f32[1024,256]{1,0:T(8,128)}, bf16[1024,256]{1,0:T(8,128)(2,1)}, bf16[1024,256]{1,0:T(8,128)(2,1)}) custom-call(bf16[64,4096]{1,0:T(8,128)(2,1)} %bitcast.8, f32[64,4096]{1,0:T(8,128)} %bitcast.6, s32[8,8,4,128]{3,2,1,0:T(4,128)} %bitcast.9, ...), custom_call_target="tpu_custom_call" | custom-call | tf_op jit(solution)/shard_map/move_rows_and_tiles/pallas_call | solution.py:373
  114.0 0.0 copy-start
  114.0 2.2 %copy-done = bf16[8,8,256,128]{3,2,1,0:T(8,128)(2,1)S(1)} copy-done((bf16[8,8,256,128]{3,2,1,0:T(8,128)(2,1)S(1)}, bf16[8,8,256,128]{3,2,1,0:T(8,128)(2,1)}, u32[]{:S(2)}) %copy-start) | copy-done | bytes 4194328
  116.2 0.0 copy-start.1
  116.2 1.2 copy-done.1
  117.4 0.0 copy-start.2
  117.4 1.0 copy-done.2
  118.5 0.0 copy-start.3
  118.5 1.0 copy-done.3
  119.5 0.0 copy-start.4
  119.5 0.8 copy-done.4
  120.3 7.1 %finish.1 = (bf16[16,128,256]{2,1,0:T(8,128)(2,1)}, bf16[1024,256]{1,0:T(8,128)(2,1)}, f32[1024,256]{1,0:T(8,128)}) custom-call(s32[8,8,128]{2,1,0:T(8,128)S(1)} %copy-done.4, bf16[8,8,256,128]{3,2,1,0:T(8,128)(2,1)S(1)} %copy-done, f32[1024,256]{1,0:T(8,128)S(1)} %copy-done.1, bf16[1024,256]{1,0:T(8,128)(2,1)S(1)} %copy-done.2, bf16[1024,256]{1,0:T(8,128)(2,1)S(1)} %copy-done.3), custom_call_target="tpu_custom_call" | custom-call | tf_op jit(solution)/shard_map/finish/pallas_call | solution.py:406
Async XLA Ops:
  114.0 2.2 %copy-start = (bf16[8,8,256,128]{3,2,1,0:T(8,128)(2,1)S(1)}, bf16[8,8,256,128]{3,2,1,0:T(8,128)(2,1)}, u32[]{:S(2)}) copy-start(bf16[8,8,256,128]{3,2,1,0:T(8,128)(2,1)} %get-tuple-element.12.arr_ref) | copy-start | bytes 12582916
  116.2 1.2 copy-start.1
  117.4 1.0 copy-start.2
  118.5 1.0 copy-start.3
  119.5 0.8 copy-start.4

commit v2 on v1

v2 whole, which is shorter than its diff:
```python
import functools
import jax
import jax.numpy as jnp
from jax import lax
from jax.experimental import pallas as pl
from jax.experimental.pallas import tpu as pltpu
from jax.sharding import PartitionSpec as P

LEARN_RATE = 0.3
EPSILON = 1e-08
MESH = pl.DeviceIdType.MESH
NY, NZ, NCORE, NX = 4, 8, 2, 4
PLANE = NY * NCORE
ROWS = 1024
DIM = 256
BAGS = 128
LOOK = 4
TILES = 16
FEAT = DIM // NX
SPAN = PLANE * BAGS
TILE_UNIT = 2048
PAIRS = NZ * PLANE
HALF = DIM // 2


def move_kernel(
    emb_ref, acc_ref, cot_ref, lens_ref, rows_ref, dest_ref, tile_ref,
    arr_ref, tiles_ref, grad_ref, own_ref, state_ref,
    emb_all, counts, cot_all, part, tile_rows, idx, msg, gsend, grecv, gsum, chosen, acc_half, acc_own, row_ids, tile_nums,
    acc_full, lens, pair_rows, dests, pair_tiles,
    ex_s, ex_r, ax_s, ax_r, ix_s, ix_r, e_s, e_r, cy_s, cy_r, cx_s, cx_r, p_s, p_r, t_s, t_r, g_s, g_r, loc,
):
    t = lax.axis_index("table")
    x = lax.axis_index("col")
    y, z, core = t // (NZ * NCORE), (t // NCORE) % NZ, t % NCORE

    def at(yy, zz, cc):
        return (lax.rem(yy + NY, NY) * NZ + lax.rem(zz + NZ, NZ)) * NCORE + lax.rem(cc + NCORE, NCORE)

    def plane(zz):
        return lax.rem(zz + 2 * NZ, NZ)

    def spot(yy, cc):
        return lax.rem(yy + NY, NY) * NCORE + lax.rem(cc + NCORE, NCORE)

    me = spot(y, core)
    others = [(dy, dc) for dy in (2, 1, 3, 0) for dc in (0, 1) if (dy, dc) != (0, 0)]

    barrier = pltpu.get_barrier_semaphore()
    for j in range(1, NX):
        pl.semaphore_signal(barrier, inc=1, device_id=(t, lax.rem(x + j, NX)), device_id_type=MESH)
    for j in range(1, NZ):
        pl.semaphore_signal(barrier, inc=1, device_id=(at(y, z + j, core), x), device_id_type=MESH)
    for dy, dc in others:
        pl.semaphore_signal(barrier, inc=1, device_id=(at(y + dy, z, core + dc), x), device_id_type=MESH)

    def local(src, dst, k):
        copy = pltpu.make_async_copy(src, dst, loc.at[k])
        copy.start()
        return copy

    def feature_rows(q):
        return pl.ds(pl.multiple_of(q * FEAT, FEAT), FEAT)

    def lanes(start, size):
        return pl.ds(pl.multiple_of(start, 128), size)

    small = [
        local(rows_ref, pair_rows, 10), local(lens_ref, lens, 11),
        local(dest_ref, dests, 12), local(tile_ref, pair_tiles, 13),
    ]
    own_rows = local(emb_ref.at[:, lanes(x * ROWS, ROWS)], emb_all.at[z, feature_rows(x)], 14)
    acc_in = local(acc_ref, acc_full, 15)
    own_cot = local(cot_ref, cot_all.at[me], 0)
    pl.semaphore_wait(barrier, NX - 1 + NZ - 1 + PLANE - 1)

    sent = []

    def send(src, dst, send_sem, recv_sem, table, col):
        copy = pltpu.make_async_remote_copy(
            src_ref=src, dst_ref=dst, send_sem=send_sem, recv_sem=recv_sem, device_id=(table, col), device_id_type=MESH
        )
        copy.start()
        sent.append(copy)

    def arrived(dst, recv_sem):
        pltpu.make_async_copy(dst, dst, recv_sem).wait()

    for j in (1, 3, 2):
        owner = lax.rem(x + j, NX)
        send(
            emb_ref.at[:, lanes(owner * ROWS, ROWS)], emb_all.at[z, feature_rows(x)],
            ex_s.at[j - 1], ex_r.at[j - 1], t, owner,
        )

    ORDER = (0, 1, 3, 2)

    def pass_rows(way, step, order, q):
        source = plane(z - step) if way == 0 else plane(z + step)
        target = plane(z + 1) if way == 0 else plane(z - 1)
        block = emb_all.at[source, feature_rows(q)]
        send(block, block, e_s.at[way, step, order], e_r.at[way, step + 1, order], at(y, target, core), x)

    def wait_rows(way, step, order, q):
        source = plane(z - step) if way == 0 else plane(z + step)
        arrived(emb_all.at[source, feature_rows(q)], e_r.at[way, step, order])

    own_rows.wait()
    for way in (0, 1):
        pass_rows(way, 0, 0, x)

    def tiles4(c):
        return pl.ds(4 * c, 4)

    for c in range(4):
        for way, dy in ((0, 1), (1, -1)):
            c_way = c if way == 0 else (c + 2) % 4
            send(
                cot_ref.at[tiles4(c_way)], cot_all.at[me, tiles4(c_way)],
                cy_s.at[way, 0, c_way], cy_r.at[way, 1, c_way], at(y + dy, z, core), x,
            )
    for c in range(4):
        send(cot_ref.at[tiles4(c)], cot_all.at[me, tiles4(c)], cx_s.at[0, c], cx_r.at[0, c], at(y, z, core + 1), x)

    for copy in small:
        copy.wait()
    place = lax.broadcasted_iota(jnp.int32, (PAIRS, PAIRS), 0)
    where_to = ((place & 7) >> 1) * (NZ * NCORE) + (place >> 3) * NCORE + (place & 1)
    match = dests[...] == where_to
    pick_pair = jnp.where(match, 1.0, 0.0).astype(jnp.bfloat16)
    pair_tile = jnp.sum(jnp.where(match, pair_tiles[...], 0), axis=1, keepdims=True)
    for l in range(LOOK):
        row = jnp.where(lens[...] > l, pair_rows[:, l, :], ROWS)
        high = (row >> 5).astype(jnp.float32).astype(jnp.bfloat16)
        low = (row & 31).astype(jnp.float32).astype(jnp.bfloat16)
        got = jnp.dot(pick_pair, high, preferred_element_type=jnp.float32) * 32.0 + jnp.dot(
            pick_pair, low, preferred_element_type=jnp.float32
        )
        msg[:, l] = (got.astype(jnp.int32) + pair_tile * TILE_UNIT).reshape(NZ, PLANE, BAGS)
    for off in (1, 7, 2, 6, 3, 5, 4):
        target = plane(z + off)
        send(msg.at[target], idx.at[z], ix_s.at[off], ix_r.at[off], at(y, target, core), x)
    idx[z] = msg[z]

    ids = lax.broadcasted_iota(jnp.int32, (DIM, BAGS), 0)
    row_ids[...] = ids.astype(jnp.float32).astype(jnp.bfloat16)

    def build(zo):
        one, zero = jnp.ones((), jnp.bfloat16), jnp.zeros((), jnp.bfloat16)

        def pair(n, carry):
            held = [idx[zo, l, pl.ds(n, 1), :] for l in range(LOOK)]
            tile_rows[n, pl.ds(zo, 1), :] = (held[0] >> 11) & (TILES - 1)
            for block in range(ROWS // DIM):
                total = None
                for l in range(LOOK):
                    near = jnp.clip((held[l] & (TILE_UNIT - 1)) - block * DIM, -1, DIM)
                    hit = jnp.where(row_ids[...] == near.astype(jnp.float32).astype(jnp.bfloat16), one, zero)
                    total = hit if total is None else total + hit
                counts[zo, pl.ds(block * DIM, DIM), lanes(n * BAGS, BAGS)] = total
            return carry

        lax.fori_loop(0, PLANE, pair, 0)

    def pool(zo):
        def block(b, carry):
            got = jnp.dot(
                emb_all[zo], counts[zo, :, lanes(b * DIM, DIM)], preferred_element_type=jnp.float32
            ).astype(jnp.bfloat16)
            part[zo, 2 * b] = got[:, :BAGS]
            part[zo, 2 * b + 1] = got[:, BAGS:]
            return carry

        lax.fori_loop(0, SPAN // DIM, block, 0)

    kept = []

    def send_part(zo, order):
        for k, (dy, dc) in enumerate(others):
            dest = spot(y + dy, core + dc)
            send(part.at[zo, dest], arr_ref.at[me, zo], p_s.at[order, k], p_r.at[order, k], at(y + dy, z, core + dc), x)
        kept.append(local(part.at[zo, me], arr_ref.at[me, zo], 1 + order))

    def relay_cot(way, step, c):
        dy = 1 if way == 0 else -1
        source = spot(y - dy * step, core)
        block = cot_all.at[source, tiles4(c)]
        arrived(block, cy_r.at[way, step, c])
        if step == 1 and c // 2 == way:
            send(block, block, cy_s.at[way, 1, c], cy_r.at[way, 2, c], at(y + dy, z, core), x)
        slot = 1 + way if step == 1 else 3
        send(block, block, cx_s.at[slot, c], cx_r.at[slot, c], at(y, z, core + 1), x)

    def gradient(zo, slot):
        def pick(n, carry):
            chosen[pl.ds(pl.multiple_of(n * BAGS, BAGS), BAGS), :] = cot_all[n, tile_nums[n, zo, 0]]
            return carry

        lax.fori_loop(0, PLANE, pick, 0)

        def block(b, carry):
            rows = pl.ds(pl.multiple_of(b * DIM, DIM), DIM)
            gsum[slot, rows, :] = jnp.dot(counts[zo, rows, :], chosen[...], preferred_element_type=jnp.float32)
            return carry

        lax.fori_loop(0, ROWS // DIM, block, 0)

    def pass_grad(way, dist, block, add, slot):
        rows = slice(block * DIM, (block + 1) * DIM)
        value = gsum[slot, rows, :]
        if add:
            arrived(grecv.at[way, dist, rows], g_r.at[way, dist, block])
            value = value + grecv[way, dist, rows, :].astype(jnp.float32)
        gsend[way, dist - 1, rows, :] = value.astype(jnp.bfloat16)
        target = plane(z + 1) if way == 0 else plane(z - 1)
        send(
            gsend.at[way, dist - 1, rows], grecv.at[way, dist - 1, rows],
            g_s.at[way, dist - 1, block], g_r.at[way, dist - 1, block], at(y, target, core), x,
        )

    zs = [z] + [plane(z - s) if w == 0 else plane(z + s) for s in (1, 2, 3) for w in (0, 1)] + [plane(z + 4)]

    def builds(step):
        for way in (0, 1) if step < 4 else (0,):
            zo = plane(z - step) if way == 0 else plane(z + step)
            arrived(idx.at[zo], ix_r.at[step if way == 0 else NZ - step])
            build(zo)

    def rows_on(step):
        for k in range(NX):
            q = lax.rem(x - ORDER[k] + NX, NX)
            for way in (0, 1):
                wait_rows(way, step, k, q)
                if step < 3 or (k < 2) == (way == 0):
                    pass_rows(way, step, k, q)

    build(z)
    for k in range(1, NX):
        j = ORDER[k]
        q = lax.rem(x - j + NX, NX)
        arrived(emb_all.at[z, feature_rows(q)], ex_r.at[j - 1])
        for way in (0, 1):
            pass_rows(way, 0, k, q)
    acc_in.wait()
    acc_half[...] = acc_full[...].astype(jnp.bfloat16)
    for j in range(1, NX):
        owner = lax.rem(x + j, NX)
        send(
            acc_half.at[:, lanes(owner * ROWS, ROWS)], acc_own.at[feature_rows(x)],
            ax_s.at[j - 1], ax_r.at[j - 1], t, owner,
        )
    acc_own[feature_rows(x), :] = acc_half[:, lanes(x * ROWS, ROWS)]
    builds(1)
    rows_on(1)
    for c in (0, 1):
        relay_cot(0, 1, c)
        relay_cot(1, 1, 2 + c)
    pool(z)
    builds(2)
    rows_on(2)
    for c in (0, 1):
        relay_cot(0, 1, 2 + c)
        relay_cot(1, 1, c)
    pool(zs[1])
    pool(zs[2])
    builds(3)
    for c in (0, 1):
        relay_cot(0, 2, c)
        relay_cot(1, 2, 2 + c)
    for order in (0, 1, 2):
        send_part(zs[order], order)
    rows_on(3)
    builds(4)

    to_scalars = local(tile_rows, tile_nums, 9)
    for k, (dy, dc) in enumerate(others):
        dest = spot(y + dy, core + dc)
        send(tile_rows.at[dest], tiles_ref.at[me], t_s.at[k], t_r.at[k], at(y + dy, z, core + dc), x)
    tiles_ref[me] = tile_rows[me]
    to_scalars.wait()

    own_cot.wait()
    for c in range(4):
        arrived(cot_all.at[spot(y, core + 1), tiles4(c)], cx_r.at[0, c])
        arrived(cot_all.at[spot(y - 1, core + 1), tiles4(c)], cx_r.at[1, c])
        arrived(cot_all.at[spot(y + 1, core + 1), tiles4(c)], cx_r.at[2, c])
        arrived(cot_all.at[spot(y + 2, core + 1), tiles4(c)], cx_r.at[3, c])

    gradient(zs[7], 0)
    for block in (0, 1):
        pass_grad(0, 4, block, False, 0)
        pass_grad(1, 4, block + 2, False, 0)
    for order in (3, 4):
        pool(zs[order])
        send_part(zs[order], order)
    early, late = ((2, 3), (0, 1)), ((0, 1), (2, 3))
    for dist in (3, 2, 1):
        for way in (0, 1):
            gradient(plane(z + dist) if way == 0 else plane(z - dist), way)
        if dist == 2:
            for order in (5, 6):
                pool(zs[order])
                send_part(zs[order], order)
        if dist == 1:
            for k in range(NX):
                wait_rows(0 if k < 2 else 1, 4, k, lax.rem(x - ORDER[k] + NX, NX))
            pool(zs[7])
            send_part(zs[7], 7)
        for blocks, add in ((early, dist < 3), (late, True)):
            for k in (0, 1):
                for way in (0, 1):
                    pass_grad(way, dist, blocks[way][k], add, way)
    gradient(z, 0)

    for j in range(1, NX):
        arrived(acc_own.at[feature_rows(lax.rem(x - j + NX, NX))], ax_r.at[j - 1])

    def turn(b, carry):
        rows = pl.ds(pl.multiple_of(b * 128, 128), 128)
        own_ref[rows, :] = emb_all[z, :, rows].astype(jnp.float32).T.astype(jnp.bfloat16)
        state_ref[rows, :] = acc_own[:, rows].astype(jnp.float32).T.astype(jnp.bfloat16)
        return carry

    lax.fori_loop(0, ROWS // 128, turn, 0)

    for way in (0, 1):
        for block in range(ROWS // DIM):
            arrived(grecv.at[way, 0, block * DIM : (block + 1) * DIM], g_r.at[way, 0, block])

    def total(b, carry):
        rows = pl.ds(pl.multiple_of(b * DIM, DIM), DIM)
        grad_ref[rows, :] = (
            gsum[0, rows, :] + grecv[0, 0, rows, :].astype(jnp.float32) + grecv[1, 0, rows, :].astype(jnp.float32)
        )
        return carry

    lax.fori_loop(0, ROWS // DIM, total, 0)

    for order, zo in enumerate(zs):
        for k, (dy, dc) in enumerate(others):
            arrived(arr_ref.at[spot(y - dy, core - dc), zo], p_r.at[order, k])
    for k, (dy, dc) in enumerate(others):
        arrived(tiles_ref.at[spot(y - dy, core - dc)], t_r.at[k])
    for copy in kept:
        copy.wait()
    for copy in sent:
        copy.wait_send()


def finish_kernel(tiles_ref, arr_ref, grad_ref, own_ref, state_ref, pooled_ref, rows_ref, sums_ref, total):
    step = pl.program_id(0)

    @pl.when(step == 0)
    def _():
        total[...] = jnp.zeros_like(total)

    def add(k, carry):
        tile = tiles_ref[step, k, 0]
        total[tile] = total[tile] + arr_ref[0, k].astype(jnp.float32)
        return carry

    lax.fori_loop(0, NZ, add, 0)
    grad = grad_ref[...]
    new_state = state_ref[...].astype(jnp.float32) + grad * grad
    sums_ref[...] = new_state
    rows_ref[...] = (
        own_ref[...].astype(jnp.float32) - LEARN_RATE * grad / (jnp.sqrt(new_state) + EPSILON)
    ).astype(jnp.bfloat16)

    @pl.when(step == PLANE - 1)
    def _():
        def turn(k, carry):
            pooled_ref[k] = total[k].T.astype(jnp.bfloat16)
            return carry

        lax.fori_loop(0, TILES, turn, 0)


def per_device(embedding, accumulator, pair_rows, pair_len, pair_dest, pair_tile, pooled_grad):
    smem = pl.BlockSpec(memory_space=pltpu.SMEM)
    vmem = pl.BlockSpec(memory_space=pltpu.VMEM)
    hbm = pl.BlockSpec(memory_space=pl.ANY)
    bf16, f32, i32 = jnp.bfloat16, jnp.float32, jnp.int32
    dma = pltpu.SemaphoreType.DMA
    sems = [(3,), (3,), (3,), (3,), (8,), (8,), (2, 5, 4), (2, 5, 4), (2, 3, 4), (2, 3, 4), (4, 4), (4, 4),
            (8, 7), (8, 7), (7,), (7,), (2, 4, 4), (2, 4, 4), (16,)]
    arr, tiles, grad, own, state = pl.pallas_call(
        move_kernel,
        out_shape=(
            jax.ShapeDtypeStruct((PLANE, NZ, DIM, BAGS), bf16),
            jax.ShapeDtypeStruct((PLANE, NZ, BAGS), i32),
            jax.ShapeDtypeStruct((ROWS, DIM), f32),
            jax.ShapeDtypeStruct((ROWS, DIM), bf16),
            jax.ShapeDtypeStruct((ROWS, DIM), bf16),
        ),
        in_specs=[hbm] * 7,
        out_specs=(hbm, vmem, vmem, vmem, vmem),
        scratch_shapes=[
            pltpu.VMEM((NZ, DIM, ROWS), bf16),
            pltpu.VMEM((NZ, ROWS, SPAN), bf16),
            pltpu.VMEM((PLANE, TILES, BAGS, DIM), bf16),
            pltpu.VMEM((NZ, PLANE, DIM, BAGS), bf16),
            pltpu.VMEM((PLANE, NZ, BAGS), i32),
            pltpu.VMEM((NZ, LOOK, PLANE, BAGS), i32),
            pltpu.VMEM((NZ, LOOK, PLANE, BAGS), i32),
            pltpu.VMEM((2, 4, ROWS, DIM), bf16),
            pltpu.VMEM((2, 4, ROWS, DIM), bf16),
            pltpu.VMEM((2, ROWS, DIM), f32),
            pltpu.VMEM((SPAN, DIM), bf16),
            pltpu.VMEM((FEAT, NX * ROWS), bf16),
            pltpu.VMEM((DIM, ROWS), bf16),
            pltpu.VMEM((DIM, BAGS), bf16),
            pltpu.SMEM((PLANE, NZ, BAGS), i32),
            pltpu.VMEM((FEAT, NX * ROWS), f32),
            pltpu.VMEM((PAIRS, BAGS), i32),
            pltpu.VMEM((PAIRS, LOOK, BAGS), i32),
            pltpu.VMEM((1, PAIRS), i32),
            pltpu.VMEM((1, PAIRS), i32),
        ]
        + [dma(s) for s in sems],
        compiler_params=pltpu.CompilerParams(collective_id=0, has_side_effects=True, vmem_limit_bytes=58 << 20),
        name="move_rows_and_tiles",
    )(
        embedding.T, accumulator.T, pooled_grad.reshape(TILES, BAGS, DIM),
        pair_len, jnp.transpose(pair_rows, (0, 2, 1)), pair_dest, pair_tile,
    )
    rows8 = ROWS // PLANE
    row_block = pl.BlockSpec((rows8, DIM), lambda i: (i, 0))
    pooled, new_rows, new_state = pl.pallas_call(
        finish_kernel,
        grid=(PLANE,),
        out_shape=(
            jax.ShapeDtypeStruct((TILES, BAGS, DIM), bf16),
            jax.ShapeDtypeStruct((ROWS, DIM), bf16),
            jax.ShapeDtypeStruct((ROWS, DIM), f32),
        ),
        in_specs=[smem, pl.BlockSpec((1, NZ, DIM, BAGS), lambda i: (i, 0, 0, 0)), row_block, row_block, row_block],
        out_specs=(pl.BlockSpec((TILES, BAGS, DIM), lambda i: (0, 0, 0)), row_block, row_block),
        scratch_shapes=[pltpu.VMEM((TILES, DIM, BAGS), f32)],
        compiler_params=pltpu.CompilerParams(vmem_limit_bytes=58 << 20),
        name="finish",
    )(tiles, arr, grad, own, state)
    return (pooled.reshape(TILES * BAGS, DIM), new_rows, new_state)


def solution(mesh):
    return jax.shard_map(
        per_device,
        mesh=mesh,
        in_specs=(
            P("table", "col"),
            P("table", "col"),
            P(("table", "col"), None, None),
            P(("table", "col"), None),
            P(("table", "col"), None),
            P(("table", "col"), None),
            P(("table", "col"), None),
        ),
        out_specs=(P(("table", "col"), None), P(("table", "col"), None), P(("table", "col"), None)),
        check_vma=False,
    )
```

time: 128 us -> 108 us (0.84)
  the two profiles are of different devices: /device:TPU:2 before, /device:TPU:1 now
where the time goes in v2:
time: 108 us; the launch traced here: 107 us
  Pallas kernels  107 us (99%)
    pallas_call x1, Pallas kernels, per_device(): pl.pallas_call(move_kernel, out_shape=(jax.ShapeDtypeStruct((PLANE, NZ, D...  97.4 us
    pallas_call x1, Pallas kernels, per_device(): pl.pallas_call(finish_kernel, grid=(PLANE,), out_shape=(jax.ShapeDtypeStr...  9.41 us

profile of v2, /device:TPU:1, one launch (start us, length us, event | category | flops | bytes accessed | tf_op | source)
XLA Modules:
  0.0 107.5 jit_solution(10599632370516036801)
XLA Ops:
  0.6 97.4 %move_rows_and_tiles.1 = (bf16[8,8,256,128]{3,2,1,0:T(8,128)(2,1)}, s32[8,8,128]{2,1,0:T(8,128)}, f32[1024,256]{1,0:T(8,128)}, bf16[1024,256]{1,0:T(8,128)(2,1)}, bf16[1024,256]{1,0:T(8,128)(2,1)}) custom-call(bf16[64,4096]{1,0:T(8,128)(2,1)} %bitcast.7, f32[64,4096]{1,0:T(8,128)} %bitcast.5, bf16[16,128,256]{2,1,0:T(8,128)(2,1)} %bitcast.6, ...), custom_call_target="tpu_custom_call" | custom-call | tf_op jit(solution)/shard_map/move_rows_and_tiles/pallas_call | solution.py:387
  98.1 9.4 %finish.1 = (bf16[16,128,256]{2,1,0:T(8,128)(2,1)}, bf16[1024,256]{1,0:T(8,128)(2,1)}, f32[1024,256]{1,0:T(8,128)}) custom-call(s32[8,8,128]{2,1,0:T(8,128)} %get-tuple-element.11.tiles_ref, bf16[8,8,256,128]{3,2,1,0:T(8,128)(2,1)} %get-tuple-element.12.arr_ref, f32[1024,256]{1,0:T(8,128)} %get-tuple-element.13.grad_ref, ...), custom_call_target="tpu_custom_call" | custom-call | tf_op jit(solution)/shard_map/finish/pallas_call | solution.py:429

commit v3 on v2

v3 whole, which is shorter than its diff:
```python
import functools
import jax
import jax.numpy as jnp
from jax import lax
from jax.experimental import pallas as pl
from jax.experimental.pallas import tpu as pltpu
from jax.sharding import PartitionSpec as P

LEARN_RATE = 0.3
EPSILON = 1e-08
MESH = pl.DeviceIdType.MESH
NY, NZ, NCORE, NX = 4, 8, 2, 4
PLANE = NY * NCORE
ROWS = 1024
DIM = 256
BAGS = 128
LOOK = 4
TILES = 16
FEAT = DIM // NX
SPAN = PLANE * BAGS
TILE_UNIT = 2048
PAIRS = NZ * PLANE
HALF = DIM // 2


def move_kernel(
    emb_ref, acc_ref, cot_ref, lens_ref, rows_ref, dest_ref, tile_ref,
    pooled_ref, new_rows_ref, new_sums_ref,
    emb_all, counts, cot_all, part, tile_rows, idx, msg, gfar, grecv, gsum, chosen, acc_half, acc_own, row_ids, tile_nums,
    acc_full, lens, pair_rows, dests, pair_tiles, arr, tiles, sums, codes, code_nums, pooled, grad, own, state,
    ex_s, ex_r, ax_s, ax_r, ix_s, ix_r, e_s, e_r, cy_s, cy_r, cx_s, cx_r, p_s, p_r, t_s, t_r, g_s, g_r, loc,
):
    t = lax.axis_index("table")
    x = lax.axis_index("col")
    y, z, core = t // (NZ * NCORE), (t // NCORE) % NZ, t % NCORE

    def at(yy, zz, cc):
        return (lax.rem(yy + NY, NY) * NZ + lax.rem(zz + NZ, NZ)) * NCORE + lax.rem(cc + NCORE, NCORE)

    def plane(zz):
        return lax.rem(zz + 2 * NZ, NZ)

    def spot(yy, cc):
        return lax.rem(yy + NY, NY) * NCORE + lax.rem(cc + NCORE, NCORE)

    me = spot(y, core)
    others = [(dy, dc) for dy in (2, 1, 3, 0) for dc in (0, 1) if (dy, dc) != (0, 0)]

    barrier = pltpu.get_barrier_semaphore()
    for j in range(1, NX):
        pl.semaphore_signal(barrier, inc=1, device_id=(t, lax.rem(x + j, NX)), device_id_type=MESH)
    for j in range(1, NZ):
        pl.semaphore_signal(barrier, inc=1, device_id=(at(y, z + j, core), x), device_id_type=MESH)
    for dy, dc in others:
        pl.semaphore_signal(barrier, inc=1, device_id=(at(y + dy, z, core + dc), x), device_id_type=MESH)

    def local(src, dst, k):
        copy = pltpu.make_async_copy(src, dst, loc.at[k])
        copy.start()
        return copy

    def feature_rows(q):
        return pl.ds(pl.multiple_of(q * FEAT, FEAT), FEAT)

    def lanes(start, size):
        return pl.ds(pl.multiple_of(start, 128), size)

    small = [
        local(rows_ref, pair_rows, 10), local(lens_ref, lens, 11),
        local(dest_ref, dests, 12), local(tile_ref, pair_tiles, 13),
    ]
    own_rows = local(emb_ref.at[:, lanes(x * ROWS, ROWS)], emb_all.at[z, feature_rows(x)], 14)
    acc_in = local(acc_ref, acc_full, 15)
    own_cot = local(cot_ref, cot_all.at[me], 0)
    pl.semaphore_wait(barrier, NX - 1 + NZ - 1 + PLANE - 1)

    sent = []

    def send(src, dst, send_sem, recv_sem, table, col):
        copy = pltpu.make_async_remote_copy(
            src_ref=src, dst_ref=dst, send_sem=send_sem, recv_sem=recv_sem, device_id=(table, col), device_id_type=MESH
        )
        copy.start()
        sent.append(copy)
        return copy

    def room(stream):
        if len(stream) == 2:
            first = stream.pop(0)
            first.wait_send()
            sent[:] = [copy for copy in sent if copy is not first]

    def arrived(dst, recv_sem):
        pltpu.make_async_copy(dst, dst, recv_sem).wait()

    for j in (1, 3, 2):
        owner = lax.rem(x + j, NX)
        send(
            emb_ref.at[:, lanes(owner * ROWS, ROWS)], emb_all.at[z, feature_rows(x)],
            ex_s.at[j - 1], ex_r.at[j - 1], t, owner,
        )

    ORDER = (0, 1, 3, 2)

    def pass_rows(way, step, order, q):
        source = plane(z - step) if way == 0 else plane(z + step)
        target = plane(z + 1) if way == 0 else plane(z - 1)
        block = emb_all.at[source, feature_rows(q)]
        return send(block, block, e_s.at[way, step, order], e_r.at[way, step + 1, order], at(y, target, core), x)

    def wait_rows(way, step, order, q):
        source = plane(z - step) if way == 0 else plane(z + step)
        arrived(emb_all.at[source, feature_rows(q)], e_r.at[way, step, order])

    row_stream, cot_stream, grad_stream = ([], []), ([], []), ([], [])

    def rows_step(i):
        step, k = i // NX, i % NX
        if i == 0:
            own_rows.wait()
        elif step == 0:
            arrived(emb_all.at[z, feature_rows(lax.rem(x - ORDER[k] + NX, NX))], ex_r.at[ORDER[k] - 1])
        for way in (0, 1):
            kk = k + 2 * way if step == 3 else k
            q = lax.rem(x - ORDER[kk] + NX, NX)
            if step:
                wait_rows(way, step, kk, q)
            room(row_stream[way])
            row_stream[way].append(pass_rows(way, step, kk, q))

    rows_step(0)

    def tiles4(c):
        return pl.ds(4 * c, 4)

    def send_cot(c):
        for way, dy in ((0, 1), (1, -1)):
            c_way = c if way == 0 else (c + 2) % 4
            room(cot_stream[way])
            cot_stream[way].append(
                send(
                    cot_ref.at[tiles4(c_way)], cot_all.at[me, tiles4(c_way)],
                    cy_s.at[way, 0, c_way], cy_r.at[way, 1, c_way], at(y + dy, z, core), x,
                )
            )

    send_cot(0)

    for copy in small:
        copy.wait()
    place = lax.broadcasted_iota(jnp.int32, (PAIRS, PAIRS), 0)
    where_to = ((place & 7) >> 1) * (NZ * NCORE) + (place >> 3) * NCORE + (place & 1)
    match = dests[...] == where_to
    pick_pair = jnp.where(match, 1.0, 0.0).astype(jnp.bfloat16)
    pair_tile = jnp.sum(jnp.where(match, pair_tiles[...], 0), axis=1, keepdims=True)
    for l in range(LOOK):
        row = jnp.where(lens[...] > l, pair_rows[:, l, :], ROWS)
        high = (row >> 5).astype(jnp.float32).astype(jnp.bfloat16)
        low = (row & 31).astype(jnp.float32).astype(jnp.bfloat16)
        got = jnp.dot(pick_pair, high, preferred_element_type=jnp.float32) * 32.0 + jnp.dot(
            pick_pair, low, preferred_element_type=jnp.float32
        )
        msg[:, l] = (got.astype(jnp.int32) + pair_tile * TILE_UNIT).reshape(NZ, PLANE, BAGS)
    for off in (1, 7, 2, 6, 3, 5, 4):
        target = plane(z + off)
        send(msg.at[target], idx.at[z], ix_s.at[off], ix_r.at[off], at(y, target, core), x)
    idx[z] = msg[z]

    ids = lax.broadcasted_iota(jnp.int32, (DIM, BAGS), 0)
    row_ids[...] = ids.astype(jnp.float32).astype(jnp.bfloat16)

    def build(zo, order):
        one, zero = jnp.ones((), jnp.bfloat16), jnp.zeros((), jnp.bfloat16)

        def pair(n, carry):
            held = [idx[zo, l, pl.ds(n, 1), :] for l in range(LOOK)]
            tile_rows[n, order : order + 1, :] = (held[0] >> 11) & (TILES - 1)
            for block in range(ROWS // DIM):
                total = None
                for l in range(LOOK):
                    near = jnp.clip((held[l] & (TILE_UNIT - 1)) - block * DIM, -1, DIM)
                    hit = jnp.where(row_ids[...] == near.astype(jnp.float32).astype(jnp.bfloat16), one, zero)
                    total = hit if total is None else total + hit
                counts[zo, pl.ds(block * DIM, DIM), lanes(n * BAGS, BAGS)] = total
            return carry

        lax.fori_loop(0, PLANE, pair, 0)

    def pool(zo):
        def block(b, carry):
            got = jnp.dot(
                emb_all[zo], counts[zo, :, lanes(b * DIM, DIM)], preferred_element_type=jnp.float32
            ).astype(jnp.bfloat16)
            part[zo, 2 * b] = got[:, :BAGS]
            part[zo, 2 * b + 1] = got[:, BAGS:]
            return carry

        lax.fori_loop(0, SPAN // DIM, block, 0)

    kept = []

    def send_part(order):
        zo = zs[order]
        for k, (dy, dc) in enumerate(others):
            dest = spot(y + dy, core + dc)
            send(part.at[zo, dest], arr.at[me, order], p_s.at[order, k], p_r.at[order, k], at(y + dy, z, core + dc), x)
        kept.append(local(part.at[zo, me], arr.at[me, order], 1 + order))

    def relay_cot(way, step, c):
        dy = 1 if way == 0 else -1
        source = spot(y - dy * step, core)
        block = cot_all.at[source, tiles4(c)]
        arrived(block, cy_r.at[way, step, c])
        if step == 1 and c // 2 == way:
            room(cot_stream[way])
            cot_stream[way].append(
                send(block, block, cy_s.at[way, 1, c], cy_r.at[way, 2, c], at(y + dy, z, core), x)
            )
        slot = 1 + way if step == 1 else 3
        send(block, block, cx_s.at[slot, c], cx_r.at[slot, c], at(y, z, core + 1), x)

    def gradient(order, slot):
        zo = zs[order]
        into = grad if slot is None else gsum.at[slot]

        def pick(n, carry):
            chosen[pl.ds(pl.multiple_of(n * BAGS, BAGS), BAGS), :] = cot_all[n, tile_nums[n, order, 0]]
            return carry

        lax.fori_loop(0, PLANE, pick, 0)

        def block(b, carry):
            rows = pl.ds(pl.multiple_of(b * DIM, DIM), DIM)
            into[rows, :] = jnp.dot(counts[zo, rows, :], chosen[...], preferred_element_type=jnp.float32)
            return carry

        lax.fori_loop(0, ROWS // DIM, block, 0)

    def pass_grad(way, dist, block, slot):
        rows = slice(block * DIM, (block + 1) * DIM)
        add = dist < 3 or (dist == 3 and (block < 2) == (way == 0))
        held = gfar.at[way] if dist == 4 else grecv.at[way, dist]
        value = gsum[slot, rows, :]
        if add:
            arrived(held.at[rows], g_r.at[way, dist, block])
            value = value + held[rows, :].astype(jnp.float32)
        room(grad_stream[way])
        spot_rows = rows if dist < 4 else slice(block % 2 * DIM, (block % 2 + 1) * DIM)
        held[spot_rows, :] = value.astype(jnp.bfloat16)
        target = plane(z + 1) if way == 0 else plane(z - 1)
        grad_stream[way].append(
            send(
                held.at[spot_rows], grecv.at[way, dist - 1, rows],
                g_s.at[way, dist - 1, block], g_r.at[way, dist - 1, block], at(y, target, core), x,
            )
        )

    early, late = ((2, 3), (0, 1)), ((0, 1), (2, 3))
    grad_steps = [(dist, blocks, k) for dist, blocks in (
        (4, late), (3, early), (3, late), (2, early), (2, late), (1, early), (1, late)
    ) for k in (0, 1)]

    def grads_step(i):
        dist, blocks, k = grad_steps[i]
        for way in (0, 1):
            pass_grad(way, dist, blocks[way][k], way if dist < 4 else 0)

    zs = [z] + [plane(z - s) if w == 0 else plane(z + s) for s in (1, 2, 3) for w in (0, 1)] + [plane(z + 4)]

    def build_next(order):
        arrived(idx.at[zs[order]], ix_r.at[(order + 1) // 2 if order % 2 else NZ - (order + 1) // 2])
        build(zs[order], order)

    def move_acc():
        acc_in.wait()
        acc_half[...] = acc_full[...].astype(jnp.bfloat16)
        for j in range(1, NX):
            owner = lax.rem(x + j, NX)
            send(
                acc_half.at[:, lanes(owner * ROWS, ROWS)], acc_own.at[feature_rows(x)],
                ax_s.at[j - 1], ax_r.at[j - 1], t, owner,
            )
        acc_own[feature_rows(x), :] = acc_half[:, lanes(x * ROWS, ROWS)]

    rows_step(1)
    send_cot(1)
    for c in range(4):
        send(cot_ref.at[tiles4(c)], cot_all.at[me, tiles4(c)], cx_s.at[0, c], cx_r.at[0, c], at(y, z, core + 1), x)
    build(z, 0)
    rows_step(2)
    move_acc()
    rows_step(3)
    send_cot(2)
    build_next(1)
    rows_step(4)
    pool(zs[0])
    send_part(0)
    rows_step(5)
    send_cot(3)
    build_next(2)
    rows_step(6)
    build_next(3)
    rows_step(7)
    relay_cot(0, 1, 0)
    relay_cot(1, 1, 2)
    build_next(4)
    rows_step(8)
    relay_cot(0, 1, 2)
    relay_cot(1, 1, 0)
    pool(zs[1])
    rows_step(9)
    relay_cot(0, 1, 1)
    relay_cot(1, 1, 3)
    pool(zs[2])
    rows_step(10)
    relay_cot(0, 1, 3)
    relay_cot(1, 1, 1)
    build_next(7)
    rows_step(11)
    build_next(5)
    relay_cot(0, 2, 0)
    relay_cot(1, 2, 2)
    rows_step(12)
    build_next(6)
    pool(zs[3])
    rows_step(13)

    to_scalars = local(tile_rows, tile_nums, 9)
    for k, (dy, dc) in enumerate(others):
        dest = spot(y + dy, core + dc)
        send(tile_rows.at[dest], tiles.at[me], t_s.at[k], t_r.at[k], at(y + dy, z, core + dc), x)
    tiles[me] = tile_rows[me]
    relay_cot(0, 2, 1)
    relay_cot(1, 2, 3)
    for order in (1, 2, 3):
        send_part(order)
    to_scalars.wait()
    own_cot.wait()
    for c in range(4):
        arrived(cot_all.at[spot(y, core + 1), tiles4(c)], cx_r.at[0, c])
        arrived(cot_all.at[spot(y - 1, core + 1), tiles4(c)], cx_r.at[1, c])
        arrived(cot_all.at[spot(y + 1, core + 1), tiles4(c)], cx_r.at[2, c])
        arrived(cot_all.at[spot(y + 2, core + 1), tiles4(c)], cx_r.at[3, c])

    gradient(7, 0)
    grads_step(0)
    gradient(5, 1)
    grads_step(1)
    gradient(6, 0)
    grads_step(2)
    pool(zs[4])
    grads_step(3)
    send_part(4)
    for k in (0, 1):
        wait_rows(0, 3, k + 2, lax.rem(x - ORDER[k + 2] + NX, NX))
        wait_rows(1, 3, k, lax.rem(x - ORDER[k] + NX, NX))
    pool(zs[5])
    grads_step(4)
    pool(zs[6])
    grads_step(5)
    send_part(5)
    gradient(4, 0)
    gradient(3, 1)
    grads_step(6)
    send_part(6)

    for k, (dy, dc) in enumerate(others):
        arrived(tiles.at[spot(y - dy, core - dc)], t_r.at[k])
    held = tiles[...].reshape(PAIRS, BAGS)
    down = lax.broadcasted_iota(jnp.int32, (PAIRS, BAGS), 0)
    across = lax.broadcasted_iota(jnp.int32, (PAIRS, BAGS), 1)
    tile_line = jnp.sum(jnp.where(down == across, held, 0), axis=0, keepdims=True)
    turn_down = ((down & 7) << 3) + (down >> 3)
    turn_across = ((across & 7) << 3) + (across >> 3)

    def last_of(found, turn):
        last = jnp.max(jnp.where(found, turn, -1), axis=1, keepdims=True)
        return jnp.broadcast_to(jnp.where(last < 0, PAIRS, last), (last.shape[0], BAGS))

    codes[:PAIRS] = last_of((tile_line == held) & (turn_across < turn_down) & (across < PAIRS), turn_across)
    codes[PAIRS:] = last_of((tile_line == down[:TILES]) & (across[:TILES] < PAIRS), turn_across[:TILES])
    to_codes = local(codes, code_nums, 16)
    sums[PAIRS] = jnp.zeros((DIM, BAGS), jnp.float32)

    grads_step(7)
    for k in range(NX):
        wait_rows(0 if k < 2 else 1, 4, k, lax.rem(x - ORDER[k] + NX, NX))
    pool(zs[7])
    grads_step(8)
    send_part(7)
    grads_step(9)
    gradient(2, 0)
    gradient(1, 1)
    grads_step(10)

    for j in range(1, NX):
        arrived(acc_own.at[feature_rows(lax.rem(x - j + NX, NX))], ax_r.at[j - 1])

    def turn(b, carry):
        rows = pl.ds(pl.multiple_of(b * 128, 128), 128)
        own[rows, :] = emb_all[z, :, rows].astype(jnp.float32).T.astype(jnp.bfloat16)
        state[rows, :] = acc_own[:, rows].astype(jnp.float32).T.astype(jnp.bfloat16)
        return carry

    lax.fori_loop(0, ROWS // 128, turn, 0)
    grads_step(11)
    to_codes.wait()

    def fold(order):
        for k, (dy, dc) in enumerate(others):
            arrived(arr.at[spot(y - dy, core - dc), order], p_r.at[order, k])
        kept[order].wait()

        def one(n, carry):
            sums[order * PLANE + n] = arr[n, order].astype(jnp.float32) + sums[code_nums[n * NZ + order, 0]]
            return carry

        lax.fori_loop(0, PLANE, one, 0)

    gradient(0, None)
    fold(0)
    fold(1)
    grads_step(12)
    fold(2)
    grads_step(13)
    for order in range(3, NZ):
        fold(order)
    outs = []

    def pool_out(k, carry):
        pooled[k] = sums[code_nums[PAIRS + k, 0]].T.astype(jnp.bfloat16)
        return carry

    for quarter in range(4):
        lax.fori_loop(4 * quarter, 4 * quarter + 4, pool_out, 0)
        outs.append(local(pooled.at[tiles4(quarter)], pooled_ref.at[tiles4(quarter)], 25 + quarter))
    for block in range(ROWS // DIM):
        rows = slice(block * DIM, (block + 1) * DIM)
        for way in (0, 1):
            arrived(grecv.at[way, 0, rows], g_r.at[way, 0, block])
        got = grad[rows, :] + grecv[0, 0, rows, :].astype(jnp.float32) + grecv[1, 0, rows, :].astype(jnp.float32)
        new_state = state[rows, :].astype(jnp.float32) + got * got
        grad[rows, :] = new_state
        own[rows, :] = (
            own[rows, :].astype(jnp.float32) - LEARN_RATE * got / (jnp.sqrt(new_state) + EPSILON)
        ).astype(jnp.bfloat16)
        outs.append(local(grad.at[rows], new_sums_ref.at[rows], 17 + block))
        outs.append(local(own.at[rows], new_rows_ref.at[rows], 21 + block))
    for copy in outs:
        copy.wait()
    for copy in sent:
        copy.wait_send()


def per_device(embedding, accumulator, pair_rows, pair_len, pair_dest, pair_tile, pooled_grad):
    hbm = pl.BlockSpec(memory_space=pl.ANY)
    bf16, f32, i32 = jnp.bfloat16, jnp.float32, jnp.int32
    dma = pltpu.SemaphoreType.DMA
    sems = [(3,), (3,), (3,), (3,), (8,), (8,), (2, 5, 4), (2, 5, 4), (2, 3, 4), (2, 3, 4), (4, 4), (4, 4),
            (8, 7), (8, 7), (7,), (7,), (2, 4, 4), (2, 4, 4), (29,)]
    pooled, new_rows, new_state = pl.pallas_call(
        move_kernel,
        out_shape=(
            jax.ShapeDtypeStruct((TILES, BAGS, DIM), bf16),
            jax.ShapeDtypeStruct((ROWS, DIM), bf16),
            jax.ShapeDtypeStruct((ROWS, DIM), f32),
        ),
        in_specs=[hbm] * 7,
        out_specs=[hbm] * 3,
        scratch_shapes=[
            pltpu.VMEM((NZ, DIM, ROWS), bf16),
            pltpu.VMEM((NZ, ROWS, SPAN), bf16),
            pltpu.VMEM((PLANE, TILES, BAGS, DIM), bf16),
            pltpu.VMEM((NZ, PLANE, DIM, BAGS), bf16),
            pltpu.VMEM((PLANE, NZ, BAGS), i32),
            pltpu.VMEM((NZ, LOOK, PLANE, BAGS), i32),
            pltpu.VMEM((NZ, LOOK, PLANE, BAGS), i32),
            pltpu.VMEM((2, ROWS // 2, DIM), bf16),
            pltpu.VMEM((2, 4, ROWS, DIM), bf16),
            pltpu.VMEM((2, ROWS, DIM), f32),
            pltpu.VMEM((SPAN, DIM), bf16),
            pltpu.VMEM((FEAT, NX * ROWS), bf16),
            pltpu.VMEM((DIM, ROWS), bf16),
            pltpu.VMEM((DIM, BAGS), bf16),
            pltpu.SMEM((PLANE, NZ, BAGS), i32),
            pltpu.VMEM((FEAT, NX * ROWS), f32),
            pltpu.VMEM((PAIRS, BAGS), i32),
            pltpu.VMEM((PAIRS, LOOK, BAGS), i32),
            pltpu.VMEM((1, PAIRS), i32),
            pltpu.VMEM((1, PAIRS), i32),
            pltpu.VMEM((PLANE, NZ, DIM, BAGS), bf16),
            pltpu.VMEM((PLANE, NZ, BAGS), i32),
            pltpu.VMEM((PAIRS + 1, DIM, BAGS), f32),
            pltpu.VMEM((PAIRS + TILES, BAGS), i32),
            pltpu.SMEM((PAIRS + TILES, BAGS), i32),
            pltpu.VMEM((TILES, BAGS, DIM), bf16),
            pltpu.VMEM((ROWS, DIM), f32),
            pltpu.VMEM((ROWS, DIM), bf16),
            pltpu.VMEM((ROWS, DIM), bf16),
        ]
        + [dma(s) for s in sems],
        compiler_params=pltpu.CompilerParams(collective_id=0, has_side_effects=True, vmem_limit_bytes=60 << 20),
        name="move_rows_and_tiles",
    )(
        embedding.T, accumulator.T, pooled_grad.reshape(TILES, BAGS, DIM),
        pair_len, jnp.transpose(pair_rows, (0, 2, 1)), pair_dest, pair_tile,
    )
    return (pooled.reshape(TILES * BAGS, DIM), new_rows, new_state)


def solution(mesh):
    return jax.shard_map(
        per_device,
        mesh=mesh,
        in_specs=(
            P("table", "col"),
            P("table", "col"),
            P(("table", "col"), None, None),
            P(("table", "col"), None),
            P(("table", "col"), None),
            P(("table", "col"), None),
            P(("table", "col"), None),
        ),
        out_specs=(P(("table", "col"), None), P(("table", "col"), None), P(("table", "col"), None)),
        check_vma=False,
    )
```

time: 108 us -> 107 us (level)
  Pallas kernels: 107 us -> 102 us
  local copies, waits for them, and re-layouts: 0 us -> 4.15 us
    pallas_call x2 -> x1, Pallas kernels: 107 us -> 102 us  [per_device(): pl.pallas_call(move_kernel, out_shape=(jax.ShapeDtypeStruct((TILES, BAGS,...]
    unnamed x0 -> x7, local copies, waits for them, and re-layouts: none -> 4.15 us
where the time goes in v3:
time: 107 us
  Pallas kernels  102 us (95%)
  local copies, waits for them, and re-layouts  4.15 us (4%)
    pallas_call x1, Pallas kernels, per_device(): pl.pallas_call(move_kernel, out_shape=(jax.ShapeDtypeStruct((TILES, BAGS,...  102 us
    unnamed x7, local copies, waits for them, and re-layouts  4.15 us

profile of v3, /device:TPU:1, one launch (start us, length us, event | category | flops | bytes accessed | tf_op | source)
XLA Modules:
  0.0 106.8 jit_solution(6078356427188723608)
XLA Ops:
  0.6 102.0 %move_rows_and_tiles.1 = (bf16[16,128,256]{2,1,0:T(8,128)(2,1)}, bf16[1024,256]{1,0:T(8,128)(2,1)}, f32[1024,256]{1,0:T(8,128)}) custom-call(bf16[64,4096]{1,0:T(8,128)(2,1)} %bitcast.8, f32[64,4096]{1,0:T(8,128)} %bitcast.5, bf16[16,128,256]{2,1,0:T(8,128)(2,1)} %bitcast.6, s32[64,128]{1,0:T(8,128)} %lens_ref.1, s32[64,4,128]{2,1,0:T(4,128)} %bitcast.9, ...), custom_call_target="tpu_custom_call" | custom-call | tf_op jit(solution)/shard_map/move_rows_and_tiles/pallas_call | solution.py:461
  102.7 0.0 copy-start.1
  102.7 0.0 copy-start
  102.7 2.4 %copy.13 = bf16[2048,256]{1,0:T(8,128)(2,1)} copy(bf16[2048,256]{1,0:T(8,128)(2,1)} %bitcast.7) | data formatting | bytes 2097152
  105.1 0.0 copy-done.1
  105.1 0.8 copy.14
  105.8 0.0 copy-done
  105.9 1.0 copy.15
Async XLA Ops:
  102.7 2.4 %copy-start.1 = (bf16[1024,256]{1,0:T(8,128)(2,1)S(1)}, bf16[1024,256]{1,0:T(8,128)(2,1)}, u32[]{:S(2)}) copy-start(bf16[1024,256]{1,0:T(8,128)(2,1)} %get-tuple-element.13) | copy-start | bytes 1572868
  102.7 3.2 %copy-start = (f32[1024,256]{1,0:T(8,128)S(1)}, f32[1024,256]{1,0:T(8,128)}, u32[]{:S(2)}) copy-start(f32[1024,256]{1,0:T(8,128)} %get-tuple-element.14) | copy-start | bytes 3145732

commit v4 on v3

--- a/solution.py
+++ b/solution.py
@@ -84,8 +84,8 @@
         sent.append(copy)
         return copy
 
-    def room(stream):
-        if len(stream) == 2:
+    def room(stream, most):
+        if len(stream) == most:
             first = stream.pop(0)
             first.wait_send()
             sent[:] = [copy for copy in sent if copy is not first]
@@ -125,7 +125,7 @@
             q = lax.rem(x - ORDER[kk] + NX, NX)
             if step:
                 wait_rows(way, step, kk, q)
-            room(row_stream[way])
+            room(row_stream[way], 3)
             row_stream[way].append(pass_rows(way, step, kk, q))
 
     rows_step(0)
@@ -136,7 +136,7 @@
     def send_cot(c):
         for way, dy in ((0, 1), (1, -1)):
             c_way = c if way == 0 else (c + 2) % 4
-            room(cot_stream[way])
+            room(cot_stream[way], 2)
             cot_stream[way].append(
                 send(
                     cot_ref.at[tiles4(c_way)], cot_all.at[me, tiles4(c_way)],
@@ -197,14 +197,12 @@
 
         lax.fori_loop(0, SPAN // DIM, block, 0)
 
-    kept = []
-
     def send_part(order):
         zo = zs[order]
         for k, (dy, dc) in enumerate(others):
             dest = spot(y + dy, core + dc)
             send(part.at[zo, dest], arr.at[me, order], p_s.at[order, k], p_r.at[order, k], at(y + dy, z, core + dc), x)
-        kept.append(local(part.at[zo, me], arr.at[me, order], 1 + order))
+        arr[me, order] = part[zo, me]
 
     def relay_cot(way, step, c):
         dy = 1 if way == 0 else -1
@@ -212,7 +210,7 @@
         block = cot_all.at[source, tiles4(c)]
         arrived(block, cy_r.at[way, step, c])
         if step == 1 and c // 2 == way:
-            room(cot_stream[way])
+            room(cot_stream[way], 2)
             cot_stream[way].append(
                 send(block, block, cy_s.at[way, 1, c], cy_r.at[way, 2, c], at(y + dy, z, core), x)
             )
@@ -244,7 +242,7 @@
         if add:
             arrived(held.at[rows], g_r.at[way, dist, block])
             value = value + held[rows, :].astype(jnp.float32)
-        room(grad_stream[way])
+        room(grad_stream[way], 3)
         spot_rows = rows if dist < 4 else slice(block % 2 * DIM, (block % 2 + 1) * DIM)
         held[spot_rows, :] = value.astype(jnp.bfloat16)
         target = plane(z + 1) if way == 0 else plane(z - 1)
@@ -294,7 +292,6 @@
     build_next(1)
     rows_step(4)
     pool(zs[0])
-    send_part(0)
     rows_step(5)
     send_cot(3)
     build_next(2)
@@ -320,10 +317,8 @@
     build_next(5)
     relay_cot(0, 2, 0)
     relay_cot(1, 2, 2)
-    rows_step(12)
     build_next(6)
     pool(zs[3])
-    rows_step(13)
 
     to_scalars = local(tile_rows, tile_nums, 9)
     for k, (dy, dc) in enumerate(others):
@@ -332,7 +327,7 @@
     tiles[me] = tile_rows[me]
     relay_cot(0, 2, 1)
     relay_cot(1, 2, 3)
-    for order in (1, 2, 3):
+    for order in (0, 1, 2, 3):
         send_part(order)
     to_scalars.wait()
     own_cot.wait()
@@ -344,8 +339,10 @@
 
     gradient(7, 0)
     grads_step(0)
+    rows_step(12)
     gradient(5, 1)
     grads_step(1)
+    rows_step(13)
     gradient(6, 0)
     grads_step(2)
     pool(zs[4])
@@ -409,7 +406,6 @@
     def fold(order):
         for k, (dy, dc) in enumerate(others):
             arrived(arr.at[spot(y - dy, core - dc), order], p_r.at[order, k])
-        kept[order].wait()
 
         def one(n, carry):
             sums[order * PLANE + n] = arr[n, order].astype(jnp.float32) + sums[code_nums[n * NZ + order, 0]]
@@ -434,7 +430,7 @@
     for quarter in range(4):
         lax.fori_loop(4 * quarter, 4 * quarter + 4, pool_out, 0)
         outs.append(local(pooled.at[tiles4(quarter)], pooled_ref.at[tiles4(quarter)], 25 + quarter))
-    for block in range(ROWS // DIM):
+    for block in (0, 2, 1, 3):
         rows = slice(block * DIM, (block + 1) * DIM)
         for way in (0, 1):
             arrived(grecv.at[way, 0, rows], g_r.at[way, 0, block])
@@ -450,6 +446,27 @@
         copy.wait()
     for copy in sent:
         copy.wait_send()
+
+
+def hand_over_kernel(pooled_in, rows_in, sums_in, pooled_ref, rows_ref, sums_ref, pooled, rows, sums, sem_in, sem_out):
+    pieces = []
+    for source, held, target, count in (
+        (pooled_in, pooled, pooled_ref, 4), (sums_in, sums, sums_ref, 4), (rows_in, rows, rows_ref, 2)
+    ):
+        size = source.shape[0] // count
+        for k in range(count):
+            part, n = pl.ds(k * size, size), len(pieces)
+            pieces.append((
+                pltpu.make_async_copy(source.at[part], held.at[part], sem_in.at[n]),
+                pltpu.make_async_copy(held.at[part], target.at[part], sem_out.at[n]),
+            ))
+    for load, _ in pieces:
+        load.start()
+    for load, store in pieces:
+        load.wait()
+        store.start()
+    for _, store in pieces:
+        store.wait()
 
 
 def per_device(embedding, accumulator, pair_rows, pair_len, pair_dest, pair_tile, pooled_grad):
@@ -505,6 +522,25 @@
         embedding.T, accumulator.T, pooled_grad.reshape(TILES, BAGS, DIM),
         pair_len, jnp.transpose(pair_rows, (0, 2, 1)), pair_dest, pair_tile,
     )
+    pooled, new_rows, new_state = pl.pallas_call(
+        hand_over_kernel,
+        out_shape=(
+            jax.ShapeDtypeStruct((TILES, BAGS, DIM), bf16),
+            jax.ShapeDtypeStruct((ROWS, DIM), bf16),
+            jax.ShapeDtypeStruct((ROWS, DIM), f32),
+        ),
+        in_specs=[hbm] * 3,
+        out_specs=[hbm] * 3,
+        scratch_shapes=[
+            pltpu.VMEM((TILES, BAGS, DIM), bf16),
+            pltpu.VMEM((ROWS, DIM), bf16),
+            pltpu.VMEM((ROWS, DIM), f32),
+            dma((10,)),
+            dma((10,)),
+        ],
+        compiler_params=pltpu.CompilerParams(vmem_limit_bytes=60 << 20),
+        name="hand_over",
+    )(pooled, new_rows, new_state)
     return (pooled.reshape(TILES * BAGS, DIM), new_rows, new_state)
 
 

time: 107 us -> 105 us (0.981)
  local copies, waits for them, and re-layouts: 4.15 us -> 0 us
  Pallas kernels: 102 us -> 104 us
    unnamed x7 -> x0, local copies, waits for them, and re-layouts: 4.15 us -> none
    pallas_call x0 -> x1, Pallas kernels: none -> 2.6 us  [per_device(): pl.pallas_call(hand_over_kernel, out_shape=(jax.ShapeDtypeStruct((TILES,...]
where the time goes in v4:
time: 105 us
  Pallas kernels  104 us (99%)
    pallas_call x1, Pallas kernels, per_device(): pl.pallas_call(move_kernel, out_shape=(jax.ShapeDtypeStruct((TILES, BAGS,...  102 us
    pallas_call x1, Pallas kernels, per_device(): pl.pallas_call(hand_over_kernel, out_shape=(jax.ShapeDtypeStruct((TILES,...  2.6 us

profile of v4, /device:TPU:1, one launch (start us, length us, event | category | flops | bytes accessed | tf_op | source)
XLA Modules:
  0.0 105.1 jit_solution(8633732966504499171)
XLA Ops:
  0.6 101.8 %move_rows_and_tiles.1 = (bf16[16,128,256]{2,1,0:T(8,128)(2,1)}, bf16[1024,256]{1,0:T(8,128)(2,1)}, f32[1024,256]{1,0:T(8,128)}) custom-call(bf16[64,4096]{1,0:T(8,128)(2,1)} %bitcast.7, f32[64,4096]{1,0:T(8,128)} %bitcast.5, bf16[16,128,256]{2,1,0:T(8,128)(2,1)} %bitcast.6, s32[64,128]{1,0:T(8,128)} %lens_ref.1, s32[64,4,128]{2,1,0:T(4,128)} %bitcast.8, ...), custom_call_target="tpu_custom_call" | custom-call | tf_op jit(solution)/shard_map/move_rows_and_tiles/pallas_call | solution.py:478
  102.5 2.6 %hand_over.1 = (bf16[16,128,256]{2,1,0:T(8,128)(2,1)}, bf16[1024,256]{1,0:T(8,128)(2,1)}, f32[1024,256]{1,0:T(8,128)}) custom-call(bf16[16,128,256]{2,1,0:T(8,128)(2,1)} %get-tuple-element.9.pooled_in, bf16[1024,256]{1,0:T(8,128)(2,1)} %get-tuple-element.10.rows_in, f32[1024,256]{1,0:T(8,128)} %get-tuple-element.11.sums_in), custom_call_target="tpu_custom_call" | custom-call | tf_op jit(solution)/shard_map/hand_over/pallas_call | solution.py:525

commit v5 on v4

--- a/solution.py
+++ b/solution.py
@@ -312,6 +312,17 @@
     rows_step(10)
     relay_cot(0, 1, 3)
     relay_cot(1, 1, 1)
+
+    for j in range(1, NX):
+        arrived(acc_own.at[feature_rows(lax.rem(x - j + NX, NX))], ax_r.at[j - 1])
+
+    def turn(b, carry):
+        rows = pl.ds(pl.multiple_of(b * 128, 128), 128)
+        own[rows, :] = emb_all[z, :, rows].astype(jnp.float32).T.astype(jnp.bfloat16)
+        state[rows, :] = acc_own[:, rows].astype(jnp.float32).T.astype(jnp.bfloat16)
+        return carry
+
+    lax.fori_loop(0, ROWS // 128, turn, 0)
     build_next(7)
     rows_step(11)
     build_next(5)
@@ -390,16 +401,6 @@
     gradient(1, 1)
     grads_step(10)
 
-    for j in range(1, NX):
-        arrived(acc_own.at[feature_rows(lax.rem(x - j + NX, NX))], ax_r.at[j - 1])
-
-    def turn(b, carry):
-        rows = pl.ds(pl.multiple_of(b * 128, 128), 128)
-        own[rows, :] = emb_all[z, :, rows].astype(jnp.float32).T.astype(jnp.bfloat16)
-        state[rows, :] = acc_own[:, rows].astype(jnp.float32).T.astype(jnp.bfloat16)
-        return carry
-
-    lax.fori_loop(0, ROWS // 128, turn, 0)
     grads_step(11)
     to_codes.wait()
 
@@ -413,12 +414,12 @@
 
         lax.fori_loop(0, PLANE, one, 0)
 
-    gradient(0, None)
     fold(0)
     fold(1)
     grads_step(12)
     fold(2)
     grads_step(13)
+    gradient(0, None)
     for order in range(3, NZ):
         fold(order)
     outs = []

time: 105 us -> 105 us (level)
  no operation moved by 1% of the time
where the time goes in v5:
time: 105 us
  Pallas kernels  104 us (99%)
    pallas_call x1, Pallas kernels, per_device(): pl.pallas_call(move_kernel, out_shape=(jax.ShapeDtypeStruct((TILES, BAGS,...  102 us
    pallas_call x1, Pallas kernels, per_device(): pl.pallas_call(hand_over_kernel, out_shape=(jax.ShapeDtypeStruct((TILES,...  2.6 us

profile of v5, /device:TPU:1, one launch (start us, length us, event | category | flops | bytes accessed | tf_op | source)
XLA Modules:
  0.0 105.1 jit_solution(7469429229928761905)
XLA Ops:
  0.6 101.8 %move_rows_and_tiles.1 = (bf16[16,128,256]{2,1,0:T(8,128)(2,1)}, bf16[1024,256]{1,0:T(8,128)(2,1)}, f32[1024,256]{1,0:T(8,128)}) custom-call(bf16[64,4096]{1,0:T(8,128)(2,1)} %bitcast.7, f32[64,4096]{1,0:T(8,128)} %bitcast.5, bf16[16,128,256]{2,1,0:T(8,128)(2,1)} %bitcast.6, s32[64,128]{1,0:T(8,128)} %lens_ref.1, s32[64,4,128]{2,1,0:T(4,128)} %bitcast.8, ...), custom_call_target="tpu_custom_call" | custom-call | tf_op jit(solution)/shard_map/move_rows_and_tiles/pallas_call | solution.py:479
  102.5 2.6 %hand_over.1 = (bf16[16,128,256]{2,1,0:T(8,128)(2,1)}, bf16[1024,256]{1,0:T(8,128)(2,1)}, f32[1024,256]{1,0:T(8,128)}) custom-call(bf16[16,128,256]{2,1,0:T(8,128)(2,1)} %get-tuple-element.9.pooled_in, bf16[1024,256]{1,0:T(8,128)(2,1)} %get-tuple-element.10.rows_in, f32[1024,256]{1,0:T(8,128)} %get-tuple-element.11.sums_in), custom_call_target="tpu_custom_call" | custom-call | tf_op jit(solution)/shard_map/hand_over/pallas_call | solution.py:526
